TPU v7x, 128 devices: a whole 4x4x4 slice. The times are simulated.
128 devices in a mesh: gx: 8 (over x, core), gy: 16 (over z, y).
Axes of the slice: x: 4, y: 4, z: 4, core: 2. Of those that a mesh axis runs over, the one named last changes fastest.
Arguments:
- features: bfloat16 [524288, 128], P(('gx', 'gy')), may hold values from -6 to 6
- weight: bfloat16 [128, 128], replicated, may hold values from -0.5 to 0.5
- stripe_owner: int32 [8], replicated, may hold values from 0 to 127
- dense_vals: bfloat16 [128, 8, 32, 128, 128], P(('gx', 'gy')), may hold values from -0.12988281 to 0.12988281
- dense_rows: int32 [128, 8, 32], P(('gx', 'gy')), may hold values from 0 to 31
- dense_cols: int32 [128, 8, 32], P(('gx', 'gy')), may hold values from 0 to 31
- sparse_vals: bfloat16 [128, 256, 128, 128], P(('gx', 'gy')), may hold values from -0.12988281 to 0.12988281
- sparse_rows: int32 [128, 256], P(('gx', 'gy')), may hold values from 0 to 31
- sparse_cols: int32 [128, 256], P(('gx', 'gy')), may hold values from 0 to 255
- requests: int32 [128, 128, 256], P(('gx', 'gy')), may hold values from 0 to 4095
- counts: int32 [128, 128], P(('gx', 'gy')), may hold values from 192 to 256, as said below
Outputs:
- aggregated: bfloat16 [524288, 128], P(('gx', 'gy'))
Inputs may be any that keep to these rules, and one draw needn't show every extreme that they name: Slots s >= counts[d, p] carry arbitrary row numbers and are not used; every requesting device has some owner with all 256 slots live.
All inputs are finite; a program needn't handle non-finite values.
Results may differ from a plain program's by a relative error of at most 0.0049.
Values may be sent and summed in bfloat16 or wider, within the bound.
No kernel may reach another device: no remote copies, remote signals or barrier semaphores. Data moves between devices by JAX's collectives and lax.ppermute only.
A program may use at most 192 MiB of HBM per device.

v0:
```python
import jax
import jax.numpy as jnp
from jax import lax
from jax.sharding import PartitionSpec as P


def broadcast(block, axis, source):
    block = jnp.where(lax.axis_index(axis) == source, block, jnp.zeros_like(block))
    return lax.psum(block, axis)


def tile_terms(total, blocks, values, targets):
    products = jnp.einsum("nbg,ngv->nbv", values, blocks, preferred_element_type=jnp.float32)
    return total.at[targets].add(products)


def local(
    features,
    weight,
    stripe_owner,
    dense_vals,
    dense_rows,
    dense_cols,
    sparse_vals,
    sparse_rows,
    sparse_cols,
    requests,
    counts,
):
    rows_dev, width = features.shape
    tile = dense_vals.shape[-1]
    row_tiles = rows_dev // tile
    rounds = dense_vals.shape[1]
    owners = requests.shape[1]
    slots = requests.shape[2]
    projected = jnp.dot(features, weight, preferred_element_type=jnp.float32).astype(jnp.bfloat16)
    wanted_rows = lax.all_to_all(requests, ("gx", "gy"), split_axis=1, concat_axis=0, tiled=True)
    selected_rows = jnp.take(projected, wanted_rows.reshape(owners, slots), axis=0)
    received = lax.all_to_all(selected_rows, ("gx", "gy"), split_axis=0, concat_axis=0, tiled=True)
    active_mask = jnp.arange(slots, dtype=jnp.int32)[None, :] < counts[0][:, None]
    received = jnp.where(active_mask[:, :, None], received, jnp.zeros_like(received))
    blocks = jnp.take(received.reshape(-1, tile, width), sparse_cols[0], axis=0)
    total = jnp.zeros((row_tiles, tile, width), jnp.float32)
    total = tile_terms(total, blocks, sparse_vals[0], sparse_rows[0])
    for step in range(rounds):
        owner = stripe_owner[step]
        stripe = broadcast(projected, ("gx", "gy"), owner)
        chosen = jnp.take(stripe.reshape(row_tiles, tile, width), dense_cols[0, step], axis=0)
        total = tile_terms(total, chosen, dense_vals[0, step], dense_rows[0, step])
    return jnp.maximum(total, 0.0).reshape(rows_dev, width).astype(jnp.bfloat16)


def solution(mesh):
    placed = (
        P(("gx", "gy"), None),
        P(),
        P(),
        P(("gx", "gy"), None, None, None, None),
        P(("gx", "gy"), None, None),
        P(("gx", "gy"), None, None),
        P(("gx", "gy"), None, None, None),
        P(("gx", "gy"), None),
        P(("gx", "gy"), None),
        P(("gx", "gy"), None, None),
        P(("gx", "gy"), None),
    )
    return jax.shard_map(
        local, mesh=mesh, in_specs=placed, out_specs=P(("gx", "gy"), None), check_vma=False
    )
```

profile of v0, /device:TPU:1, one launch (start us, length us, event | category | flops | bytes accessed | tf_op | source)
XLA Modules:
  0.0 586.7 jit_solution(3814535602601073258)
XLA Ops:
  6.5 1.8 copy.58
  8.3 11.5 %all-to-all-start = ((s32[1,128,256]{2,0,1:T(1,128)}), s32[1,128,256]{2,0,1:T(1,128)S(1)}, u32[]{:S(2)}, u32[]{:S(2)}) async-start(s32[1,128,256]{2,0,1:T(1,128)} %copy.58), calls=%async_computation | async-start | bytes 262144 | tf_op jit(solution)/shard_map/all_to_all | solution.py:37
  19.8 1.6 fusion.61
  26.4 5.1 broadcast_select_fusion.2
  31.7 114.2 %gather_fusion = bf16[32768,128]{1,0:T(8,128)(2,1)} fusion(bf16[4096,128]{1,0:T(8,128)(2,1)S(1)} %get-tuple-element.68, s32[32768]{0:T(1024)S(1)} %broadcast_clamp_fusion), kind=kCustom, calls=%fused_computation.8 | custom fusion | bytes 16908288 | tf_op jit(solution)/shard_map/jit(_take)/gather | solution.py:38
  146.0 7.6 %broadcast_select_fusion = bf16[128,256,128]{2,1,0:T(8,128)(2,1)} fusion(bf16[128,256,128]{2,1,0:T(8,128)(2,1)} %bitcast.137, pred[128,256]{1,0:T(8,128)(4,1)S(1)} %compare_and_fusion), kind=kLoop, calls=%fused_computation.23 | loop fusion | flops 4194304 | bytes 16809984 | tf_op jit(solution)/shard_map/jit(_take)/select_n | solution.py:38
  153.6 10.2 %all-to-all-start.1 = ((bf16[128,256,128]{2,1,0:T(8,128)(2,1)}), bf16[128,256,128]{2,1,0:T(8,128)(2,1)}, u32[]{:S(2)}, u32[]{:S(2)}) async-start(bf16[128,256,128]{2,1,0:T(8,128)(2,1)} %broadcast_select_fusion), calls=%async_computation.1 | async-start | bytes 16777216 | tf_op jit(solution)/shard_map/all_to_all | solution.py:39
  164.1 0.4 all-reduce.3.cloned.1.call-update
  165.0 244.0 %all-reduce.3.cloned.1.call-done = (bf16[32,128,128]{2,1,0:T(8,128)(2,1)}, bf16[32,128,128]{2,1,0:T(8,128)(2,1)}, bf16[32,128,128]{2,1,0:T(8,128)(2,1)}, bf16[32...) async-done(((bf16[32,128,128]{2,1,0:T(8,128)(2,1)}, ...) | async-done | bytes 8388624 | tf_op jit(solution)/shard_map/psum | solution.py:9
  408.9 2.0 gather_fusion.2
  410.9 2.2 convolution_bitcast_fusion.8
  413.2 1.8 copy.62
  415.0 2.0 gather_fusion.3
  417.0 2.2 convolution_bitcast_fusion.7
  419.2 1.9 copy.64
  421.1 2.0 gather_fusion.4
  423.0 2.2 convolution_bitcast_fusion.6
  425.3 1.8 copy.66
  427.1 2.0 gather_fusion.5
  429.1 2.2 convolution_bitcast_fusion.5
  431.3 1.8 copy.68
  433.1 2.0 gather_fusion.6
  435.1 2.2 convolution_bitcast_fusion.4
  437.3 1.9 copy.70
  439.2 2.0 gather_fusion.7
  441.2 2.2 convolution_bitcast_fusion.3
  443.4 1.8 copy.72
  445.2 2.0 gather_fusion.8
  447.2 2.2 convolution_bitcast_fusion.2
  449.4 1.9 copy.74
  451.3 2.0 gather_fusion.9
  453.2 2.2 convolution_bitcast_fusion.1
  455.5 1.8 copy.76
  457.3 7.6 %broadcast_select_fusion.1 = bf16[128,256,128]{2,1,0:T(8,128)(2,1)} fusion(bf16[128,256,128]{2,1,0:T(8,128)(2,1)} %all-to-all-done.1, pred[128,256]{1,0:T(8,128)(4,1)S(1)} %iota_compare_fusion), kind=kLoop, calls=%fused_computation.24 | loop fusion | flops 4194304 | bytes 16809984 | tf_op jit(solution)/shard_map/jit(_where)/select_n | solution.py:41
  464.9 12.2 %gather_fusion.1 = bf16[256,128,128]{2,1,0:T(8,128)(2,1)} fusion(bf16[256,128,128]{2,1,0:T(8,128)(2,1)} %bitcast.138, s32[1024]{0:T(1024)S(1)} %pad_clamp_fusion.8), kind=kCustom, calls=%fused_computation.9 | custom fusion | bytes 16778240 | tf_op jit(solution)/shard_map/jit(_take)/gather | solution.py:42
  477.1 13.2 %convolution_bitcast_fusion = f32[256,128,128]{1,2,0:T(8,128)} fusion(bf16[1,256,128,128]{3,2,1,0:T(8,128)(2,1)} %param.19, bf16[256,128,128]{2,1,0:T(8,128)(2,1)} %gather_fusion.1, pred[256]{0:T(512)(128)(4,1)S(1)} %compare_and_fusion.9), kind=kOutput, calls=%fused_computation.19 | convolution fusion | flops 1077936128 | bytes 33554688 | tf_op jit(solution)/shard_map/nbg,ngv->nbv/dot_general | solution.py:13
  490.3 17.5 %copy.60 = f32[256,128,128]{2,1,0:T(8,128)} copy(f32[256,128,128]{1,2,0:T(8,128)} %convolution_bitcast_fusion) | data formatting | bytes 33554432 | tf_op jit(solution)/shard_map/nbg,ngv->nbv/dot_general | solution.py:13
  507.8 0.2 broadcast.202
  508.0 33.2 %scatter_fusion = f32[32,128,128]{2,1,0:T(8,128)S(1)} fusion(f32[32,128,128]{2,1,0:T(8,128)S(1)} %broadcast.202, s32[256]{0:T(256)S(1)} %bitcast.148, f32[256,128,128]{2,1,0:T(8,128)} %copy.60), kind=kCustom, calls=%fused_computation.10 | custom fusion | flops 4194304 | bytes 50332672 | tf_op jit(solution)/shard_map/scatter-add | solution.py:14
  541.2 4.7 scatter_fusion.1
  545.9 4.7 scatter_fusion.2
  550.6 4.7 scatter_fusion.3
  555.3 4.7 scatter_fusion.4
  559.9 4.7 scatter_fusion.5
  564.6 4.7 scatter_fusion.6
  569.3 4.7 scatter_fusion.7
  574.0 4.7 scatter_fusion.8
  578.7 1.2 maximum_convert_fusion
  (31 shorter events, 0.8 us)
Async XLA Ops:
  6.5 19.9 %copy-start = (bf16[4096,128]{1,0:T(8,128)(2,1)S(1)}, bf16[4096,128]{1,0:T(8,128)(2,1)}, u32[]{:S(2)}) copy-start(bf16[4096,128]{1,0:T(8,128)(2,1)} %param.13) | copy-start | bytes 3145732
  8.3 23.3 %all-to-all-start = ((s32[1,128,256]{2,0,1:T(1,128)}), s32[1,128,256]{2,0,1:T(1,128)S(1)}, u32[]{:S(2)}, u32[]{:S(2)}) async-start(s32[1,128,256]{2,0,1:T(1,128)} %copy.58), calls=%async_computation | async-start | bytes 262144 | tf_op jit(solution)/shard_map/all_to_all | solution.py:37
  153.6 303.7 %all-to-all-start.1 = ((bf16[128,256,128]{2,1,0:T(8,128)(2,1)}), bf16[128,256,128]{2,1,0:T(8,128)(2,1)}, u32[]{:S(2)}, u32[]{:S(2)}) async-start(bf16[128,256,128]{2,1,0:T(8,128)(2,1)} %broadcast_select_fusion), calls=%async_computation.1 | async-start | bytes 16777216 | tf_op jit(solution)/shard_map/all_to_all | solution.py:39
  163.8 245.1 %all-reduce.3.cloned.1.call-start = ((), (), s32[]{:S(2)}) async-start(), calls=%async_computation.2 | async-start | bytes 16777216 | tf_op jit(solution)/shard_map/psum | solution.py:9
  164.0 0.7 copy-start.4
  164.0 0.7 copy-start.2
  164.1 0.8 copy-start.5
  164.1 0.8 copy-start.3
  164.1 0.8 copy-start.6
  574.0 5.9 %copy-start.1 = (bf16[4096,128]{1,0:T(8,128)(2,1)S(1)}, bf16[4096,128]{1,0:T(8,128)(2,1)}, u32[]{:S(2)}) copy-start(bf16[4096,128]{1,0:T(8,128)(2,1)} %param.13) | copy-start | bytes 3145732
Sparse Core Ops, SparseCore 0:
  171.0 237.8 all-reduce.2
where the time goes:
time: 589 us; the launch traced here: 587 us
  waiting for transfers between devices  244 us (41%)
  local copies, waits for them, and re-layouts  178 us (30%)
  other arithmetic  87.4 us (15%)
  matrix products  36.1 us (6%)
  starting transfers between devices  21.9 us (4%)
  between operations  18.8 us (3%)
    psum x1, waiting for transfers between devices, broadcast(): return lax.psum(block, axis)  244 us
    gather x1, local copies, waits for them, and re-layouts, local(): jnp.take(projected, wanted_rows.reshape(owners, slots), axis=0)  114 us
    scatter-add x9, other arithmetic, tile_terms(): return total.at[targets].add(products)  70.6 us
    dot_general x9, local copies, waits for them, and re-layouts, tile_terms(): jnp.einsum('nbg,ngv->nbv', values, blocks, preferred_element_type=jnp.flo...  32.2 us
    dot_general x9, matrix products, tile_terms(): jnp.einsum('nbg,ngv->nbv', values, blocks, preferred_element_type=jnp.flo...  30.9 us
    gather x8, local copies, waits for them, and re-layouts, local(): jnp.take(stripe.reshape(row_tiles, tile, width), dense_cols[0, step], axi...  15.8 us
    gather x1, local copies, waits for them, and re-layouts, local(): blocks = jnp.take(received.reshape(-1, tile, width), sparse_cols[0], axis=0)  12.2 us
  transfers between devices with their start and end apart: 3, of which 1 were waited for; matrix products, arithmetic and copies ran while one was open for 9% of the time, Pallas kernels for 0%

commit v1 on v0

v1 whole, which is shorter than its diff:
```python
import jax
import jax.numpy as jnp
from jax import lax
from jax.experimental import pallas as pl
from jax.experimental.pallas import tpu as pltpu
from jax.sharding import PartitionSpec as P

AXES = ("gx", "gy")
LEAD = 8
GROUP = 128
VMEM = 56 * 1024 * 1024


def gather_kernel(index_ref, table_ref, out_ref, wide_ref):
    nodes = table_ref.shape[0]
    count = out_ref.shape[0]
    base = pl.program_id(0) * count

    @pl.when(pl.program_id(0) == 0)
    def _():
        wide_ref[pl.ds(LEAD, nodes), :] = table_ref[...].astype(jnp.float32)
        wide_ref[pl.ds(LEAD + nodes, 8), :] = jnp.zeros((8, 128), jnp.float32)

    sublane = lax.broadcasted_iota(jnp.int32, (8, 128), 0)
    masks = [sublane == j for j in range(8)]

    def group(step, carry):
        start = pl.multiple_of(step * GROUP, GROUP)
        parts = []
        for eight in range(GROUP // 8):
            rows = None
            for j in range(8):
                at = index_ref[base + start + eight * 8 + j]
                found = wide_ref[pl.ds(at - j, 8), :]
                rows = found if rows is None else jnp.where(masks[j], found, rows)
            parts.append(rows)
        out_ref[pl.ds(start, GROUP), :] = jnp.concatenate(parts, axis=0).astype(jnp.bfloat16)
        return carry

    lax.fori_loop(0, count // GROUP, group, 0)


def gather_rows(wanted, projected, rows_step=2048):
    count = wanted.shape[0]
    nodes, width = projected.shape
    return pl.pallas_call(
        gather_kernel,
        grid_spec=pltpu.PrefetchScalarGridSpec(
            num_scalar_prefetch=1,
            grid=(count // rows_step,),
            in_specs=[pl.BlockSpec((nodes, width), lambda i, w: (0, 0))],
            out_specs=pl.BlockSpec((rows_step, width), lambda i, w: (i, 0)),
            scratch_shapes=[pltpu.VMEM((LEAD + nodes + 8, width), jnp.float32)],
        ),
        out_shape=jax.ShapeDtypeStruct((count, width), jnp.bfloat16),
        compiler_params=pltpu.CompilerParams(vmem_limit_bytes=VMEM),
        name="gather_rows",
    )(wanted, projected)


def dense_kernel(rows_ref, cols_ref, source_ref, values_ref, total_ref):
    step = pl.program_id(0)
    tiles = values_ref.shape[0]

    @pl.when(step == 0)
    def _():
        total_ref[...] = jnp.zeros_like(total_ref)

    stripe = step * tiles // 32
    for j in range(tiles):
        row = rows_ref[step * tiles + j]
        col = cols_ref[step * tiles + j]
        block = source_ref[pl.ds(col * 4, 4), stripe].reshape(128, 128)
        product = jnp.dot(values_ref[j], block, preferred_element_type=jnp.float32)
        at = pl.ds(pl.multiple_of(row * 128, 128), 128)
        total_ref[at, :] += product


def dense_sum(rows, cols, source, values, row_tiles, tiles=16):
    count = values.shape[0]
    return pl.pallas_call(
        dense_kernel,
        grid_spec=pltpu.PrefetchScalarGridSpec(
            num_scalar_prefetch=2,
            grid=(count // tiles,),
            in_specs=[
                pl.BlockSpec(source.shape, lambda i, r, c: (0, 0, 0, 0), pipeline_mode=pl.Buffered(1)),
                pl.BlockSpec((tiles, 128, 128), lambda i, r, c: (i, 0, 0)),
            ],
            out_specs=pl.BlockSpec((row_tiles * 128, 128), lambda i, r, c: (0, 0)),
        ),
        out_shape=jax.ShapeDtypeStruct((row_tiles * 128, 128), jnp.float32),
        compiler_params=pltpu.CompilerParams(vmem_limit_bytes=VMEM),
        name="dense_sum",
    )(rows, cols, source, values)


def sparse_kernel(rows_ref, cols_ref, source_ref, values_ref, begin_ref, out_ref, total_ref):
    step = pl.program_id(0)
    tiles = values_ref.shape[0]

    @pl.when(step == 0)
    def _():
        total_ref[...] = begin_ref[...]

    for j in range(tiles):
        row = rows_ref[step * tiles + j]
        col = cols_ref[step * tiles + j]
        block = source_ref[col]
        product = jnp.dot(values_ref[j], block, preferred_element_type=jnp.float32)
        at = pl.ds(pl.multiple_of(row * 128, 128), 128)
        total_ref[at, :] += product

    @pl.when(step == pl.num_programs(0) - 1)
    def _():
        out_ref[...] = jnp.maximum(total_ref[...], 0.0).astype(jnp.bfloat16)


def sparse_sum(rows, cols, source, values, begin, tiles=16):
    count = values.shape[0]
    return pl.pallas_call(
        sparse_kernel,
        grid_spec=pltpu.PrefetchScalarGridSpec(
            num_scalar_prefetch=2,
            grid=(count // tiles,),
            in_specs=[
                pl.BlockSpec(source.shape, lambda i, r, c: (0, 0, 0), pipeline_mode=pl.Buffered(1)),
                pl.BlockSpec((tiles, 128, 128), lambda i, r, c: (i, 0, 0)),
                pl.BlockSpec(begin.shape, lambda i, r, c: (0, 0), pipeline_mode=pl.Buffered(1)),
            ],
            out_specs=pl.BlockSpec(begin.shape, lambda i, r, c: (0, 0)),
            scratch_shapes=[pltpu.VMEM(begin.shape, jnp.float32)],
        ),
        out_shape=jax.ShapeDtypeStruct(begin.shape, jnp.bfloat16),
        compiler_params=pltpu.CompilerParams(vmem_limit_bytes=VMEM),
        name="sparse_sum",
    )(rows, cols, source, values, begin)


def local(
    features,
    weight,
    stripe_owner,
    dense_vals,
    dense_rows,
    dense_cols,
    sparse_vals,
    sparse_rows,
    sparse_cols,
    requests,
    counts,
):
    rows_dev, width = features.shape
    tile = dense_vals.shape[-1]
    row_tiles = rows_dev // tile
    owners = requests.shape[1]
    slots = requests.shape[2]
    piece = rows_dev // owners
    live = jnp.arange(slots, dtype=jnp.int32)[None, :] < counts[0][:, None]
    asked = jnp.where(live, requests[0] + LEAD, rows_dev + LEAD).reshape(owners, slots // width, width)
    projected = jnp.dot(features, weight, preferred_element_type=jnp.float32).astype(jnp.bfloat16)
    message = jnp.concatenate(
        [
            projected.reshape(owners, piece, width),
            (asked // 128).astype(jnp.bfloat16),
            (asked % 128).astype(jnp.bfloat16),
        ],
        axis=1,
    )
    message = lax.all_to_all(message, AXES, split_axis=0, concat_axis=0, tiled=True)
    digits = message[:, piece:].astype(jnp.int32).reshape(owners, 2, slots)
    wanted = (digits[:, 0] * 128 + digits[:, 1]).reshape(-1)
    mine = jnp.take(message[:, :piece], stripe_owner, axis=0)
    stripes = lax.all_gather(mine[None], AXES, axis=0, tiled=True)
    selected = gather_rows(wanted, projected).reshape(owners, slots, width)
    received = lax.all_to_all(selected, AXES, split_axis=0, concat_axis=0, tiled=True)
    total = dense_sum(
        dense_rows.reshape(-1), dense_cols.reshape(-1), stripes, dense_vals.reshape(-1, tile, tile), row_tiles
    )
    return sparse_sum(
        sparse_rows.reshape(-1), sparse_cols.reshape(-1), received.reshape(-1, tile, width), sparse_vals[0], total
    )


def solution(mesh):
    placed = (
        P(AXES, None),
        P(),
        P(),
        P(AXES, None, None, None, None),
        P(AXES, None, None),
        P(AXES, None, None),
        P(AXES, None, None, None),
        P(AXES, None),
        P(AXES, None),
        P(AXES, None, None),
        P(AXES, None),
    )
    return jax.shard_map(
        local, mesh=mesh, in_specs=placed, out_specs=P(AXES, None), check_vma=False
    )
```

time: 589 us -> 235 us (0.40)
  the two profiles are of different devices: /device:TPU:1 before, /device:TPU:51 now
where the time goes in v1:
time: 235 us; the launch traced here: 234 us
  waiting for transfers between devices  123 us (52%)
  Pallas kernels  65.7 us (28%)
  starting transfers between devices  21.2 us (9%)
  between operations  13.5 us (6%)
  other arithmetic  5.21 us (2%)
  local copies, waits for them, and re-layouts  4.41 us (2%)
    all_gather x1, waiting for transfers between devices, local(): stripes = lax.all_gather(mine[None], AXES, axis=0, tiled=True)  106 us
    pallas_call x1, Pallas kernels, gather_rows(): pl.pallas_call(gather_kernel, grid_spec=pltpu.PrefetchScalarGridSpec(num_...  32.9 us
    all_to_all x1, waiting for transfers between devices, local(): lax.all_to_all(message, AXES, split_axis=0, concat_axis=0, tiled=True)  17 us
    pallas_call x1, Pallas kernels, sparse_sum(): pl.pallas_call(sparse_kernel, grid_spec=pltpu.PrefetchScalarGridSpec(num_...  16.5 us
    pallas_call x1, Pallas kernels, dense_sum(): pl.pallas_call(dense_kernel, grid_spec=pltpu.PrefetchScalarGridSpec(num_s...  16.3 us
    all_to_all x1, starting transfers between devices, local(): lax.all_to_all(selected, AXES, split_axis=0, concat_axis=0, tiled=True)  10.7 us
    all_to_all x1, starting transfers between devices, local(): lax.all_to_all(message, AXES, split_axis=0, concat_axis=0, tiled=True)  10.4 us
  transfers between devices with their start and end apart: 3, of which 2 were waited for; matrix products, arithmetic and copies ran while one was open for 1% of the time, Pallas kernels for 21%

profile of v1, /device:TPU:51, one launch (start us, length us, event | category | flops | bytes accessed | tf_op | source)
XLA Modules:
  0.0 234.1 jit_solution(12339542023301123821)
XLA Ops:
  6.5 0.0 copy-start
  6.5 1.0 broadcast_add_fusion
  7.5 0.1 add.34
  7.6 1.1 fusion.1
  8.7 0.1 fusion
  8.8 0.0 copy-done
  8.9 1.2 convolution_convert_fusion.table_ref
  10.0 0.0 copy-start.1
  10.1 0.0 copy-start.4
  10.1 1.4 pad_maximum_fusion
  11.5 10.4 %all-to-all-start = ((bf16[128,36,128]{2,1,0:T(8,128)(2,1)}), bf16[128,36,128]{2,1,0:T(8,128)(2,1)S(1)}, u32[]{:S(2)}, u32[]{:S(2)}) async-start(bf16[128,36,128]{2,1,0:T(8,128)(2,1)} %pad_maximum_fusion), calls=%async_computation | async-start | bytes 2621440 | tf_op jit(solution)/shard_map/all_to_all | solution.py:170
  21.9 0.0 all-gather.2.cloned.1.call-start
  22.0 0.0 copy-done.4
  22.0 17.0 %all-to-all-done = bf16[128,36,128]{2,1,0:T(8,128)(2,1)S(1)} async-done(((bf16[128,36,128]{2,1,0:T(8,128)(2,1)}), bf16[128,36,128]{2,1,0:T(8,128)(2,1)S(1)}, u32[]{:S(2)}, u32[]{:S(2)}) %all-to-all-start) | async-done | bytes 1179680 | tf_op jit(solution)/shard_map/all_to_all | solution.py:170
  39.0 1.1 slice.21
  40.0 0.0 copy-done.1
  40.0 1.8 gather_fusion
  41.8 0.7 bitcast_select_fusion
  42.5 0.0 all-gather.2.cloned.1.call-update
  42.5 0.1 slice_convert_fusion
  42.6 0.2 reshape.78
  42.8 0.8 slice_add_fusion
  43.6 32.9 %gather_rows.1 = bf16[32768,128]{1,0:T(8,128)(2,1)} custom-call(s32[32768]{0:T(1024)} %bitcast.17, bf16[4096,128]{1,0:T(8,128)(2,1)} %copy-done.1), custom_call_target="tpu_custom_call" | custom-call | tf_op jit(solution)/shard_map/gather_rows/pallas_call | solution.py:46
  76.5 0.0 copy-start.2
  76.5 0.0 copy-start.3
  76.5 10.7 %all-to-all-start.1 = ((bf16[128,256,128]{2,1,0:T(8,128)(2,1)}), bf16[128,256,128]{2,1,0:T(8,128)(2,1)}, u32[]{:S(2)}, u32[]{:S(2)}) async-start(bf16[128,256,128]{2,1,0:T(8,128)(2,1)} %bitcast.13), calls=%async_computation.1 | async-start | bytes 16777216 | tf_op jit(solution)/shard_map/all_to_all | solution.py:176
  87.2 0.0 copy-done.2
  87.2 0.6 reshape.74.rows_ref
  87.9 0.0 copy-done.3
  87.9 0.6 reshape.75.cols_ref
  88.5 105.9 %all-gather.2.cloned.1.call-done.source_ref = bf16[128,8,32,128]{3,2,1,0:T(8,128)(2,1)} async-done(((bf16[1,8,32,128]{3,2,1,0:T(8,128)(2,1)}), bf16[128,8,32,128]{3,2,1,0:T(8,128)(2,1)}) %all-gather.2.cloned.1.call-update) | async-done | bytes 8388624 | tf_op jit(solution)/shard_map/all_gather | solution.py:174
  194.4 16.3 %dense_sum.1.begin_ref = f32[4096,128]{1,0:T(8,128)} custom-call(s32[256]{0:T(256)} %reshape.74.rows_ref, s32[256]{0:T(256)} %reshape.75.cols_ref, bf16[128,8,32,128]{3,2,1,0:T(8,128)(2,1)} %all-gather.2.cloned.1.call-done.source_ref, bf16[256,128,128]{2,1,0:T(8,128)(2,1)} %bitcast.15), custom_call_target="tpu_custom_call" | custom-call | tf_op jit(solution)/shard_map/dense_sum/pallas_call | solution.py:81
  210.7 0.0 all-to-all-done.1
  210.7 16.5 %sparse_sum.1 = bf16[4096,128]{1,0:T(8,128)(2,1)} custom-call(s32[256]{0:T(256)} %bitcast.18, s32[256]{0:T(256)} %bitcast.19, bf16[256,128,128]{2,1,0:T(8,128)(2,1)} %bitcast.6.source_ref, bf16[256,128,128]{2,1,0:T(8,128)(2,1)} %bitcast.16, f32[4096,128]{1,0:T(8,128)} %dense_sum.1.begin_ref), custom_call_target="tpu_custom_call" | custom-call | tf_op jit(solution)/shard_map/sparse_sum/pallas_call | solution.py:121
  (4 shorter events, 0.0 us)
Async XLA Ops:
  6.5 2.3 copy-start
  10.0 30.0 %copy-start.1 = (bf16[4096,128]{1,0:T(8,128)(2,1)}, bf16[4096,128]{1,0:T(8,128)(2,1)S(1)}, u32[]{:S(2)}) copy-start(bf16[4096,128]{1,0:T(8,128)(2,1)S(1)} %convolution_convert_fusion.table_ref) | copy-start | bytes 3145732
  10.1 11.9 %copy-start.4 = (s32[8]{0:T(128)S(1)}, s32[8]{0:T(128)}, u32[]{:S(2)}) copy-start(s32[8]{0:T(128)} %param.13) | copy-start | bytes 100
  11.5 27.5 %all-to-all-start = ((bf16[128,36,128]{2,1,0:T(8,128)(2,1)}), bf16[128,36,128]{2,1,0:T(8,128)(2,1)S(1)}, u32[]{:S(2)}, u32[]{:S(2)}) async-start(bf16[128,36,128]{2,1,0:T(8,128)(2,1)} %pad_maximum_fusion), calls=%async_computation | async-start | bytes 2621440 | tf_op jit(solution)/shard_map/all_to_all | solution.py:170
  21.9 172.5 %all-gather.2.cloned.1.call-start = ((), (), s32[]{:S(2)}) async-start(), calls=%async_computation.2 | async-start | bytes 8454144 | tf_op jit(solution)/shard_map/all_gather | solution.py:174
  76.5 10.7 %copy-start.2 = (s32[1,8,32]{2,1,0:T(8,128)S(1)}, s32[1,8,32]{2,1,0:T(8,128)}, u32[]{:S(2)}) copy-start(s32[1,8,32]{2,1,0:T(8,128)} %param.15) | copy-start | bytes 3076
  76.5 11.4 %copy-start.3 = (s32[1,8,32]{2,1,0:T(8,128)S(1)}, s32[1,8,32]{2,1,0:T(8,128)}, u32[]{:S(2)}) copy-start(s32[1,8,32]{2,1,0:T(8,128)} %param.16) | copy-start | bytes 3076
  76.5 134.2 %all-to-all-start.1 = ((bf16[128,256,128]{2,1,0:T(8,128)(2,1)}), bf16[128,256,128]{2,1,0:T(8,128)(2,1)}, u32[]{:S(2)}, u32[]{:S(2)}) async-start(bf16[128,256,128]{2,1,0:T(8,128)(2,1)} %bitcast.13), calls=%async_computation.1 | async-start | bytes 16777216 | tf_op jit(solution)/shard_map/all_to_all | solution.py:176
Sparse Core Ops, SparseCore 0:
  42.7 151.7 all-gather.1

commit v2 on v0

v2 whole, which is shorter than its diff:
```python
import functools

import jax
import jax.numpy as jnp
from jax import lax
from jax.experimental import pallas as pl
from jax.experimental.pallas import tpu as pltpu
from jax.sharding import PartitionSpec as P

AXES = ("gx", "gy")
LEAD = 8
VMEM = 56 * 1024 * 1024
UNROLL = 8
LOADS = 8


def gather_kernel(index_ref, table_ref, out_ref, wide_ref, *, half, halves):
    nodes = table_ref.shape[0]
    owners, tile, width = out_ref.shape
    first = pl.program_id(0) * owners

    @pl.when(pl.program_id(0) == 0)
    def _():
        wide_ref[pl.ds(LEAD, nodes), :] = table_ref[...].astype(jnp.float32)
        wide_ref[pl.ds(LEAD + nodes, 8), :] = jnp.zeros((8, width), jnp.float32)

    sublane = lax.broadcasted_iota(jnp.int32, (8, width), 0)
    masks = [sublane == j for j in range(8)]

    def one_owner(owner, carry):
        start = ((first + owner) * halves + half) * tile
        parts = []
        for eight in range(tile // 8):
            rows = None
            for j in range(8):
                at = index_ref[start + eight * 8 + j]
                found = wide_ref[pl.ds(at - j, 8), :]
                rows = found if rows is None else jnp.where(masks[j], found, rows)
            parts.append(rows)
        out_ref[owner] = jnp.concatenate(parts, axis=0).astype(jnp.bfloat16)
        return carry

    lax.fori_loop(0, owners, one_owner, 0)


def gather_rows(wanted, projected, half, halves, owners, owners_step=16):
    nodes, width = projected.shape
    tile = wanted.shape[0] // owners // halves
    return pl.pallas_call(
        functools.partial(gather_kernel, half=half, halves=halves),
        grid_spec=pltpu.PrefetchScalarGridSpec(
            num_scalar_prefetch=1,
            grid=(owners // owners_step,),
            in_specs=[pl.BlockSpec((nodes, width), lambda i, w: (0, 0))],
            out_specs=pl.BlockSpec((owners_step, tile, width), lambda i, w: (i, 0, 0)),
            scratch_shapes=[pltpu.VMEM((LEAD + nodes + 8, width), jnp.float32)],
        ),
        out_shape=jax.ShapeDtypeStruct((owners, tile, width), jnp.bfloat16),
        compiler_params=pltpu.CompilerParams(vmem_limit_bytes=VMEM),
        name="gather_rows",
    )(wanted, projected)


def value_copy(values_ref, held_ref, sems, part):
    size = held_ref.shape[0] // LOADS
    at = pl.ds(part * size, size)
    return pltpu.make_async_copy(values_ref.at[at], held_ref.at[at], sems.at[part])


def dense_kernel(
    rows_ref, cols_ref, source_hbm, values_ref, begin_ref, total_ref, source_ref, held_ref, sems, value_sems
):
    load_source = pltpu.make_async_copy(source_hbm, source_ref, sems.at[0])
    load_begin = pltpu.make_async_copy(begin_ref, total_ref, sems.at[1])
    load_source.start()
    load_begin.start()
    for part in range(LOADS):
        value_copy(values_ref, held_ref, value_sems, part).start()
    load_begin.wait()
    load_source.wait()
    count, tile, _ = held_ref.shape
    size = count // LOADS
    pieces, stripes, piece, _ = source_ref.shape
    per_tile = tile // piece

    def group(step, carry):
        @pl.when(step % (size // UNROLL) == 0)
        def _():
            value_copy(values_ref, held_ref, value_sems, step // (size // UNROLL)).wait()

        stripe = step // (count // stripes // UNROLL)
        for j in range(UNROLL):
            k = step * UNROLL + j
            block = source_ref[pl.ds(cols_ref[k] * per_tile, per_tile), stripe].reshape(tile, tile)
            product = jnp.dot(held_ref[k], block, preferred_element_type=jnp.float32)
            at = pl.ds(pl.multiple_of(rows_ref[k] * tile, tile), tile)
            total_ref[at, :] += product
        return carry

    lax.fori_loop(0, count // UNROLL, group, 0)


def dense_sum(rows, cols, source, values, begin):
    hbm = pl.BlockSpec(memory_space=pl.ANY)
    return pl.pallas_call(
        dense_kernel,
        grid_spec=pltpu.PrefetchScalarGridSpec(
            num_scalar_prefetch=2,
            grid=(1,),
            in_specs=[hbm] * 3,
            out_specs=pl.BlockSpec(begin.shape, lambda i, r, c: (0, 0)),
            scratch_shapes=[
                pltpu.VMEM(source.shape, jnp.bfloat16),
                pltpu.VMEM(values.shape, jnp.bfloat16),
                pltpu.SemaphoreType.DMA((2,)),
                pltpu.SemaphoreType.DMA((LOADS,)),
            ],
        ),
        out_shape=jax.ShapeDtypeStruct(begin.shape, jnp.float32),
        compiler_params=pltpu.CompilerParams(vmem_limit_bytes=VMEM),
        name="dense_sum",
    )(rows, cols, source, values, begin)


def sparse_kernel(rows_ref, cols_ref, source_hbm, values_ref, *refs, half, halves, last):
    out_ref, source_ref, held_ref, total_ref, list_ref, sems, value_sems = refs[-7:]
    nodes = out_ref.shape[0]
    count = held_ref.shape[0]
    load_source = pltpu.make_async_copy(source_hbm, source_ref, sems.at[0])
    load_source.start()
    if last:
        load_begin = pltpu.make_async_copy(refs[0], total_ref.at[pl.ds(0, nodes)], sems.at[1])
        load_begin.start()
    else:
        total_ref[...] = jnp.zeros_like(total_ref)
    for part in range(LOADS):
        value_copy(values_ref, held_ref, value_sems, part).start()

    def choose(k, taken):
        list_ref[taken] = k
        return taken + jnp.where(cols_ref[k] % halves == half, 1, 0)

    taken = lax.fori_loop(0, count, choose, 0, unroll=8)
    load_source.wait()
    if last:
        load_begin.wait()
    size = count // LOADS

    def wait_part(part, carry):
        value_copy(values_ref, held_ref, value_sems, part).wait()
        return carry

    def group(step, ready):
        last_k = list_ref[jnp.minimum(step * UNROLL + UNROLL, taken) - 1]
        need = last_k // size + 1
        lax.fori_loop(ready, need, wait_part, 0)
        for j in range(UNROLL):
            entry = step * UNROLL + j
            real = entry < taken
            k = jnp.where(real, list_ref[jnp.minimum(entry, taken - 1)], last_k)
            row = jnp.where(real, rows_ref[k], nodes // 128)
            block = source_ref[cols_ref[k] // halves]
            product = jnp.dot(held_ref[k], block, preferred_element_type=jnp.float32)
            at = pl.ds(pl.multiple_of(row * 128, 128), 128)
            total_ref[at, :] += product
        return jnp.maximum(ready, need)

    ready = lax.fori_loop(0, pl.cdiv(taken, UNROLL), group, 0)
    lax.fori_loop(ready, LOADS, wait_part, 0)
    result = total_ref[pl.ds(0, nodes), :]
    if last:
        result = jnp.maximum(result, 0.0)
    out_ref[...] = result.astype(out_ref.dtype)


def sparse_sum(rows, cols, source, values, nodes, half, halves, begin=None):
    hbm = pl.BlockSpec(memory_space=pl.ANY)
    shape = (nodes, source.shape[-1])
    last = begin is not None
    more = [begin] if last else []
    return pl.pallas_call(
        functools.partial(sparse_kernel, half=half, halves=halves, last=last),
        grid_spec=pltpu.PrefetchScalarGridSpec(
            num_scalar_prefetch=2,
            grid=(1,),
            in_specs=[hbm] * (2 + len(more)),
            out_specs=pl.BlockSpec(shape, lambda i, r, c: (0, 0)),
            scratch_shapes=[
                pltpu.VMEM(source.shape, jnp.bfloat16),
                pltpu.VMEM(values.shape, jnp.bfloat16),
                pltpu.VMEM((nodes + 128, shape[1]), jnp.float32),
                pltpu.SMEM((values.shape[0] + 8,), jnp.int32),
                pltpu.SemaphoreType.DMA((2,)),
                pltpu.SemaphoreType.DMA((LOADS,)),
            ],
        ),
        out_shape=jax.ShapeDtypeStruct(shape, jnp.bfloat16 if last else jnp.float32),
        compiler_params=pltpu.CompilerParams(vmem_limit_bytes=VMEM),
        name="sparse_sum",
    )(rows, cols, source, values, *more)


def local(
    features,
    weight,
    stripe_owner,
    dense_vals,
    dense_rows,
    dense_cols,
    sparse_vals,
    sparse_rows,
    sparse_cols,
    requests,
    counts,
):
    rows_dev, width = features.shape
    tile = dense_vals.shape[-1]
    owners = requests.shape[1]
    slots = requests.shape[2]
    halves = slots // tile
    piece = rows_dev // owners
    projected = jnp.dot(features, weight, preferred_element_type=jnp.float32).astype(jnp.bfloat16)
    pieces = lax.all_to_all(
        projected.reshape(owners, piece, width), AXES, split_axis=0, concat_axis=0, tiled=True
    )
    mine = jnp.take(pieces, stripe_owner, axis=0)
    live = jnp.arange(slots, dtype=jnp.int32)[None, :] < counts[0][:, None]
    asked = jnp.where(live, requests[0] + LEAD, rows_dev + LEAD)
    asked, mine = lax.optimization_barrier((asked, mine))
    stripes = lax.all_gather(mine[None], AXES, axis=0, tiled=True)
    wanted = lax.all_to_all(asked, AXES, split_axis=0, concat_axis=0, tiled=True).reshape(-1)
    selected = gather_rows(wanted, projected, 0, halves, owners)
    selected, wanted = lax.optimization_barrier((selected, wanted))
    received = lax.all_to_all(selected, AXES, split_axis=0, concat_axis=0, tiled=True)
    selected = gather_rows(wanted, projected, 1, halves, owners)
    total = sparse_sum(sparse_rows[0], sparse_cols[0], received, sparse_vals[0], rows_dev, 0, halves)
    received = lax.all_to_all(selected, AXES, split_axis=0, concat_axis=0, tiled=True)
    total = dense_sum(
        dense_rows.reshape(-1), dense_cols.reshape(-1), stripes, dense_vals.reshape(-1, tile, tile), total
    )
    return sparse_sum(sparse_rows[0], sparse_cols[0], received, sparse_vals[0], rows_dev, 1, halves, total)


def solution(mesh):
    lead = lambda rank: P(AXES, *([None] * (rank - 1)))
    placed = (
        lead(2), P(), P(), lead(5), lead(3), lead(3), lead(4), lead(2), lead(2), lead(3), lead(2),
    )
    return jax.shard_map(local, mesh=mesh, in_specs=placed, out_specs=lead(2), check_vma=False)
```

time: 589 us -> 219 us (0.37)
  local copies, waits for them, and re-layouts: 178 us -> 3.17 us
  waiting for transfers between devices: 244 us -> 84.5 us
  other arithmetic: 87.4 us -> 0.81 us
  Pallas kernels: 0 us -> 76 us
  matrix products: 36.1 us -> 2.15 us
  blocking collectives: 0 us -> 15.4 us
    psum x1 -> x0, waiting for transfers between devices: 244 us -> none  [broadcast(): return lax.psum(block, axis)]
    gather x10 -> x1, local copies, waits for them, and re-layouts: 142 us -> 0.56 us  [local(): mine = jnp.take(pieces, stripe_owner, axis=0)]
    all_to_all x2 -> x3, waiting for transfers between devices: 0.01 us -> 84.5 us  [the longest x2 65.9 us: local(): lax.all_to_all(selected, AXES, split_axis=0, concat_axis=0, tiled=True)]
    pallas_call x0 -> x5, Pallas kernels: none -> 76 us  [the longest x2 37.9 us: gather_rows(): pl.pallas_call(functools.partial(gather_kernel, half=half, halves=halves)...]
    scatter-add x9 -> x0, other arithmetic: 70.6 us -> none  [tile_terms(): return total.at[targets].add(products)]
    dot_general x9 -> x0, local copies, waits for them, and re-layouts: 32.2 us -> none  [tile_terms(): jnp.einsum('nbg,ngv->nbv', values, blocks, preferred_element_type=jnp.flo...]
    dot_general x9 -> x0, matrix products: 30.9 us -> none  [tile_terms(): jnp.einsum('nbg,ngv->nbv', values, blocks, preferred_element_type=jnp.flo...]
    all_to_all x0 -> x1, blocking collectives: none -> 15.4 us  [local(): lax.all_to_all(asked, AXES, split_axis=0, concat_axis=0, tiled=True)]
  transfers between devices with their start and end apart: 3 -> 4, of which waited for: 1 -> 3; matrix products, arithmetic and copies ran while one was open for 9% -> 1% of each run, Pallas kernels for 0% -> 30%
where the time goes in v2:
time: 219 us; the launch traced here: 218 us
  waiting for transfers between devices  84.5 us (39%)
  Pallas kernels  76 us (35%)
  starting transfers between devices  22.5 us (10%)
  blocking collectives  15.4 us (7%)
  between operations  13.5 us (6%)
  local copies, waits for them, and re-layouts  3.17 us (1%)
    all_to_all x2, waiting for transfers between devices, local(): lax.all_to_all(selected, AXES, split_axis=0, concat_axis=0, tiled=True)  65.9 us
    pallas_call x2, Pallas kernels, gather_rows(): pl.pallas_call(functools.partial(gather_kernel, half=half, halves=halves)...  37.9 us
    pallas_call x2, Pallas kernels, sparse_sum(): pl.pallas_call(functools.partial(sparse_kernel, half=half, halves=halves,...  22.1 us
    all_to_all x1, waiting for transfers between devices, local(): lax.all_to_all(projected.reshape(owners, piece, width), AXES, split_axis=...  18.6 us
    pallas_call x1, Pallas kernels, dense_sum(): pl.pallas_call(dense_kernel, grid_spec=pltpu.PrefetchScalarGridSpec(num_s...  16 us
    all_to_all x1, blocking collectives, local(): lax.all_to_all(asked, AXES, split_axis=0, concat_axis=0, tiled=True)  15.4 us
    all_to_all x1, starting transfers between devices, local(): lax.all_to_all(projected.reshape(owners, piece, width), AXES, split_axis=...  11.5 us
    all_to_all x2, starting transfers between devices, local(): lax.all_to_all(selected, AXES, split_axis=0, concat_axis=0, tiled=True)  11 us
  transfers between devices with their start and end apart: 4, of which 3 were waited for; matrix products, arithmetic and copies ran while one was open for 1% of the time, Pallas kernels for 30%

profile of v2, /device:TPU:1, one launch (start us, length us, event | category | flops | bytes accessed | tf_op | source)
XLA Modules:
  0.0 218.1 jit_solution(16796673240863194379)
XLA Ops:
  6.5 0.0 copy-start
  6.5 0.0 copy-start.5
  6.5 0.0 copy-start.4
  6.5 0.0 copy-start.1
  6.5 1.2 copy-done
  7.8 2.1 convolution_convert_fusion.table_ref
  9.9 11.5 %all-to-all-start = ((bf16[128,32,128]{2,1,0:T(8,128)(2,1)}), bf16[128,32,128]{2,1,0:T(8,128)(2,1)S(1)}, u32[]{:S(2)}, u32[]{:S(2)}) async-start(bf16[128,32,128]{2,1,0:T(8,128)(2,1)} %bitcast.4), calls=%async_computation | async-start | bytes 2097152 | tf_op jit(solution)/shard_map/all_to_all | solution.py:223
  21.4 0.0 all-gather.3.cloned.1.call-start
  21.5 0.0 copy-done.5
  21.5 0.0 copy-done.4
  21.5 0.0 copy-done.1
  21.5 0.1 bitcast_select_fusion
  21.6 18.6 %all-to-all-done = bf16[128,32,128]{2,1,0:T(8,128)(2,1)S(1)} async-done(((bf16[128,32,128]{2,1,0:T(8,128)(2,1)}), bf16[128,32,128]{2,1,0:T(8,128)(2,1)S(1)}, u32[]{:S(2)}, u32[]{:S(2)}) %all-to-all-start) | async-done | bytes 1048608 | tf_op jit(solution)/shard_map/all_to_all | solution.py:223
  40.2 0.6 gather_fusion
  40.8 0.7 broadcast_select_fusion
  41.5 0.0 all-gather.3.cloned.1.call-update
  41.5 0.1 all_to_all.16
  41.6 15.4 %all_to_all.24 = s32[128,1,256]{2,1,0:T(1,128)} all-to-all(s32[128,1,256]{2,1,0:T(1,128)S(1)} %all_to_all.16), channel_id=1, replica_groups=mesh['gx'=8,'gy'=16] {'gx','gy'}, dimensions={0} | all-to-all | bytes 262144 | tf_op jit(solution)/shard_map/all_to_all | solution.py:231
  57.0 18.9 %gather_rows.2 = bf16[128,128,128]{2,1,0:T(8,128)(2,1)} custom-call(s32[32768]{0:T(1024)} %bitcast.16, bf16[4096,128]{1,0:T(8,128)(2,1)} %convolution_convert_fusion.table_ref), custom_call_target="tpu_custom_call" | custom-call | tf_op jit(solution)/shard_map/gather_rows/pallas_call | solution.py:49
  75.9 5.1 %all-to-all-start.3 = ((bf16[128,128,128]{2,1,0:T(8,128)(2,1)}), bf16[128,128,128]{2,1,0:T(8,128)(2,1)}, u32[]{:S(2)}, u32[]{:S(2)}) async-start(bf16[128,128,128]{2,1,0:T(8,128)(2,1)} %gather_rows.2), calls=%async_computation.3 | async-start | bytes 8388608 | tf_op jit(solution)/shard_map/all_to_all | solution.py:234
  81.0 19.0 %gather_rows.3 = bf16[128,128,128]{2,1,0:T(8,128)(2,1)} custom-call(s32[32768]{0:T(1024)} %bitcast.17, bf16[4096,128]{1,0:T(8,128)(2,1)} %convolution_convert_fusion.table_ref), custom_call_target="tpu_custom_call" | custom-call | tf_op jit(solution)/shard_map/gather_rows/pallas_call | solution.py:49
  100.0 0.0 copy-start.2
  100.0 0.0 copy-start.3
  100.0 43.4 %all-to-all-done.3.source_hbm = bf16[128,128,128]{2,1,0:T(8,128)(2,1)} async-done(((bf16[128,128,128]{2,1,0:T(8,128)(2,1)}), bf16[128,128,128]{2,1,0:T(8,128)(2,1)}, u32[]{:S(2)}, u32[]{:S(2)}) %all-to-all-start.3) | async-done | bytes 4194336 | tf_op jit(solution)/shard_map/all_to_all | solution.py:234
  143.4 5.9 %all-to-all-start.2 = ((bf16[128,128,128]{2,1,0:T(8,128)(2,1)}), bf16[128,128,128]{2,1,0:T(8,128)(2,1)}, u32[]{:S(2)}, u32[]{:S(2)}) async-start(bf16[128,128,128]{2,1,0:T(8,128)(2,1)} %gather_rows.3), calls=%async_computation.2 | async-start | bytes 8388608 | tf_op jit(solution)/shard_map/all_to_all | solution.py:237
  149.3 0.0 copy-done.2
  149.3 0.6 reshape.28.rows_ref
  149.9 0.0 copy-done.3
  150.0 0.6 reshape.29.cols_ref
  150.6 10.8 %sparse_sum.2.begin_ref = f32[4096,128]{1,0:T(8,128)} custom-call(s32[256]{0:T(256)} %bitcast.18, s32[256]{0:T(256)} %bitcast.20, bf16[128,128,128]{2,1,0:T(8,128)(2,1)} %all-to-all-done.3.source_hbm, bf16[256,128,128]{2,1,0:T(8,128)(2,1)} %bitcast.12), custom_call_target="tpu_custom_call" | custom-call | tf_op jit(solution)/shard_map/sparse_sum/pallas_call | solution.py:181
  161.4 0.0 all-gather.3.cloned.1.call-done
  161.4 16.0 %dense_sum.1.refs_0_ = f32[4096,128]{1,0:T(8,128)} custom-call(s32[256]{0:T(256)} %reshape.28.rows_ref, s32[256]{0:T(256)} %reshape.29.cols_ref, bf16[128,8,32,128]{3,2,1,0:T(8,128)(2,1)} %bitcast.15, bf16[256,128,128]{2,1,0:T(8,128)(2,1)} %bitcast.14, f32[4096,128]{1,0:T(8,128)} %sparse_sum.2.begin_ref), custom_call_target="tpu_custom_call" | custom-call | tf_op jit(solution)/shard_map/dense_sum/pallas_call | solution.py:105
  177.5 22.5 %all-to-all-done.2.source_hbm = bf16[128,128,128]{2,1,0:T(8,128)(2,1)} async-done(((bf16[128,128,128]{2,1,0:T(8,128)(2,1)}), bf16[128,128,128]{2,1,0:T(8,128)(2,1)}, u32[]{:S(2)}, u32[]{:S(2)}) %all-to-all-start.2) | async-done | bytes 4194336 | tf_op jit(solution)/shard_map/all_to_all | solution.py:237
  200.0 11.3 %sparse_sum.3 = bf16[4096,128]{1,0:T(8,128)(2,1)} custom-call(s32[256]{0:T(256)} %bitcast.19, s32[256]{0:T(256)} %bitcast.21, bf16[128,128,128]{2,1,0:T(8,128)(2,1)} %all-to-all-done.2.source_hbm, bf16[256,128,128]{2,1,0:T(8,128)(2,1)} %bitcast.13, f32[4096,128]{1,0:T(8,128)} %dense_sum.1.refs_0_), custom_call_target="tpu_custom_call" | custom-call | tf_op jit(solution)/shard_map/sparse_sum/pallas_call | solution.py:181
  (3 shorter events, 0.0 us)
Async XLA Ops:
  6.5 1.2 copy-start
  6.5 14.9 %copy-start.5 = (s32[8]{0:T(128)S(1)}, s32[8]{0:T(128)}, u32[]{:S(2)}) copy-start(s32[8]{0:T(128)} %param.13) | copy-start | bytes 100
  6.5 15.0 %copy-start.4 = (s32[1,128]{1,0:T(1,128)S(1)}, s32[1,128]{1,0:T(1,128)}, u32[]{:S(2)}) copy-start(s32[1,128]{1,0:T(1,128)} %param.21) | copy-start | bytes 1540
  6.5 15.0 %copy-start.1 = (s32[1,128,256]{2,1,0:T(8,128)S(1)}, s32[1,128,256]{2,1,0:T(8,128)}, u32[]{:S(2)}) copy-start(s32[1,128,256]{2,1,0:T(8,128)} %param.20) | copy-start | bytes 393220
  9.9 30.3 %all-to-all-start = ((bf16[128,32,128]{2,1,0:T(8,128)(2,1)}), bf16[128,32,128]{2,1,0:T(8,128)(2,1)S(1)}, u32[]{:S(2)}, u32[]{:S(2)}) async-start(bf16[128,32,128]{2,1,0:T(8,128)(2,1)} %bitcast.4), calls=%async_computation | async-start | bytes 2097152 | tf_op jit(solution)/shard_map/all_to_all | solution.py:223
  21.4 140.0 %all-gather.3.cloned.1.call-start = ((), (), s32[]{:S(2)}) async-start(), calls=%async_computation.4 | async-start | bytes 8454144 | tf_op jit(solution)/shard_map/all_gather | solution.py:230
  75.9 67.4 %all-to-all-start.3 = ((bf16[128,128,128]{2,1,0:T(8,128)(2,1)}), bf16[128,128,128]{2,1,0:T(8,128)(2,1)}, u32[]{:S(2)}, u32[]{:S(2)}) async-start(bf16[128,128,128]{2,1,0:T(8,128)(2,1)} %gather_rows.2), calls=%async_computation.3 | async-start | bytes 8388608 | tf_op jit(solution)/shard_map/all_to_all | solution.py:234
  100.0 49.3 %copy-start.2 = (s32[1,8,32]{2,1,0:T(8,128)S(1)}, s32[1,8,32]{2,1,0:T(8,128)}, u32[]{:S(2)}) copy-start(s32[1,8,32]{2,1,0:T(8,128)} %param.15) | copy-start | bytes 3076
  100.0 50.0 %copy-start.3 = (s32[1,8,32]{2,1,0:T(8,128)S(1)}, s32[1,8,32]{2,1,0:T(8,128)}, u32[]{:S(2)}) copy-start(s32[1,8,32]{2,1,0:T(8,128)} %param.16) | copy-start | bytes 3076
  143.4 56.6 %all-to-all-start.2 = ((bf16[128,128,128]{2,1,0:T(8,128)(2,1)}), bf16[128,128,128]{2,1,0:T(8,128)(2,1)}, u32[]{:S(2)}, u32[]{:S(2)}) async-start(bf16[128,128,128]{2,1,0:T(8,128)(2,1)} %gather_rows.3), calls=%async_computation.2 | async-start | bytes 8388608 | tf_op jit(solution)/shard_map/all_to_all | solution.py:237
Sparse Core Ops, SparseCore 0:
  41.7 99.2 all-gather.2

commit v3 on v2

--- a/solution.py
+++ b/solution.py
@@ -10,18 +10,21 @@
 AXES = ("gx", "gy")
 LEAD = 8
 VMEM = 56 * 1024 * 1024
-UNROLL = 8
-LOADS = 8
-
-
-def gather_kernel(index_ref, table_ref, out_ref, wide_ref, *, half, halves):
-    nodes = table_ref.shape[0]
+UNROLL = 32
+LOADS = 4
+EARLY = 24
+
+
+def gather_kernel(index_ref, features_ref, weight_ref, *refs, half, halves, first_owner):
+    out_ref, wide_ref = refs[-2:]
+    nodes = features_ref.shape[0]
     owners, tile, width = out_ref.shape
-    first = pl.program_id(0) * owners
+    first = first_owner + pl.program_id(0) * owners
 
     @pl.when(pl.program_id(0) == 0)
     def _():
-        wide_ref[pl.ds(LEAD, nodes), :] = table_ref[...].astype(jnp.float32)
+        projected = jnp.dot(features_ref[...], weight_ref[...], preferred_element_type=jnp.float32)
+        wide_ref[pl.ds(LEAD, nodes), :] = projected.astype(jnp.bfloat16).astype(jnp.float32)
         wide_ref[pl.ds(LEAD + nodes, 8), :] = jnp.zeros((8, width), jnp.float32)
 
     sublane = lax.broadcasted_iota(jnp.int32, (8, width), 0)
@@ -43,22 +46,29 @@
     lax.fori_loop(0, owners, one_owner, 0)
 
 
-def gather_rows(wanted, projected, half, halves, owners, owners_step=16):
-    nodes, width = projected.shape
+def gather_rows(wanted, features, weight, half, halves, owners, begin, end, earlier=None, owners_step=8):
+    nodes, width = features.shape
     tile = wanted.shape[0] // owners // halves
+    first = begin // owners_step
+    more = [] if earlier is None else [earlier]
     return pl.pallas_call(
-        functools.partial(gather_kernel, half=half, halves=halves),
+        functools.partial(gather_kernel, half=half, halves=halves, first_owner=begin),
         grid_spec=pltpu.PrefetchScalarGridSpec(
             num_scalar_prefetch=1,
-            grid=(owners // owners_step,),
-            in_specs=[pl.BlockSpec((nodes, width), lambda i, w: (0, 0))],
-            out_specs=pl.BlockSpec((owners_step, tile, width), lambda i, w: (i, 0, 0)),
+            grid=((end - begin) // owners_step,),
+            in_specs=[
+                pl.BlockSpec((nodes, width), lambda i, w: (0, 0)),
+                pl.BlockSpec((width, width), lambda i, w: (0, 0)),
+            ]
+            + [pl.BlockSpec(memory_space=pl.ANY) for _ in more],
+            out_specs=pl.BlockSpec((owners_step, tile, width), lambda i, w: (first + i, 0, 0)),
             scratch_shapes=[pltpu.VMEM((LEAD + nodes + 8, width), jnp.float32)],
         ),
         out_shape=jax.ShapeDtypeStruct((owners, tile, width), jnp.bfloat16),
+        input_output_aliases={3: 0} if more else {},
         compiler_params=pltpu.CompilerParams(vmem_limit_bytes=VMEM),
         name="gather_rows",
-    )(wanted, projected)
+    )(wanted, features, weight, *more)
 
 
 def value_copy(values_ref, held_ref, sems, part):
@@ -68,15 +78,15 @@
 
 
 def dense_kernel(
-    rows_ref, cols_ref, source_hbm, values_ref, begin_ref, total_ref, source_ref, held_ref, sems, value_sems
+    rows_ref, cols_ref, source_hbm, values_ref, begin_hbm, total_ref, source_ref, held_ref, begin_ref, sems, value_sems
 ):
     load_source = pltpu.make_async_copy(source_hbm, source_ref, sems.at[0])
-    load_begin = pltpu.make_async_copy(begin_ref, total_ref, sems.at[1])
+    load_begin = pltpu.make_async_copy(begin_hbm, begin_ref, sems.at[1])
     load_source.start()
-    load_begin.start()
     for part in range(LOADS):
         value_copy(values_ref, held_ref, value_sems, part).start()
-    load_begin.wait()
+    load_begin.start()
+    total_ref[...] = jnp.zeros_like(total_ref)
     load_source.wait()
     count, tile, _ = held_ref.shape
     size = count // LOADS
@@ -98,6 +108,8 @@
         return carry
 
     lax.fori_loop(0, count // UNROLL, group, 0)
+    load_begin.wait()
+    total_ref[...] += begin_ref[...]
 
 
 def dense_sum(rows, cols, source, values, begin):
@@ -112,6 +124,7 @@
             scratch_shapes=[
                 pltpu.VMEM(source.shape, jnp.bfloat16),
                 pltpu.VMEM(values.shape, jnp.bfloat16),
+                pltpu.VMEM(begin.shape, jnp.float32),
                 pltpu.SemaphoreType.DMA((2,)),
                 pltpu.SemaphoreType.DMA((LOADS,)),
             ],
@@ -123,18 +136,17 @@
 
 
 def sparse_kernel(rows_ref, cols_ref, source_hbm, values_ref, *refs, half, halves, last):
-    out_ref, source_ref, held_ref, total_ref, list_ref, sems, value_sems = refs[-7:]
+    out_ref, source_ref, held_ref, total_ref, begin_ref, list_ref, sems, value_sems = refs[-8:]
     nodes = out_ref.shape[0]
     count = held_ref.shape[0]
     load_source = pltpu.make_async_copy(source_hbm, source_ref, sems.at[0])
     load_source.start()
-    if last:
-        load_begin = pltpu.make_async_copy(refs[0], total_ref.at[pl.ds(0, nodes)], sems.at[1])
-        load_begin.start()
-    else:
-        total_ref[...] = jnp.zeros_like(total_ref)
     for part in range(LOADS):
         value_copy(values_ref, held_ref, value_sems, part).start()
+    if last:
+        load_begin = pltpu.make_async_copy(refs[0], begin_ref, sems.at[1])
+        load_begin.start()
+    total_ref[...] = jnp.zeros_like(total_ref)
 
     def choose(k, taken):
         list_ref[taken] = k
@@ -142,8 +154,6 @@
 
     taken = lax.fori_loop(0, count, choose, 0, unroll=8)
     load_source.wait()
-    if last:
-        load_begin.wait()
     size = count // LOADS
 
     def wait_part(part, carry):
@@ -169,7 +179,8 @@
     lax.fori_loop(ready, LOADS, wait_part, 0)
     result = total_ref[pl.ds(0, nodes), :]
     if last:
-        result = jnp.maximum(result, 0.0)
+        load_begin.wait()
+        result = jnp.maximum(result + begin_ref[...], 0.0)
     out_ref[...] = result.astype(out_ref.dtype)
 
 
@@ -189,6 +200,7 @@
                 pltpu.VMEM(source.shape, jnp.bfloat16),
                 pltpu.VMEM(values.shape, jnp.bfloat16),
                 pltpu.VMEM((nodes + 128, shape[1]), jnp.float32),
+                pltpu.VMEM(shape if last else (8, shape[1]), jnp.float32),
                 pltpu.SMEM((values.shape[0] + 8,), jnp.int32),
                 pltpu.SemaphoreType.DMA((2,)),
                 pltpu.SemaphoreType.DMA((LOADS,)),
@@ -219,20 +231,31 @@
     slots = requests.shape[2]
     halves = slots // tile
     piece = rows_dev // owners
-    projected = jnp.dot(features, weight, preferred_element_type=jnp.float32).astype(jnp.bfloat16)
-    pieces = lax.all_to_all(
-        projected.reshape(owners, piece, width), AXES, split_axis=0, concat_axis=0, tiled=True
+    live = jnp.arange(slots, dtype=jnp.int32)[None, :] < counts[0][:, None]
+    asked = jnp.where(live, requests[0] + LEAD, rows_dev + LEAD).reshape(owners, halves, tile)
+    message = jnp.concatenate(
+        [
+            features.reshape(owners, piece, width),
+            (asked // 128).astype(jnp.bfloat16),
+            (asked % 128).astype(jnp.bfloat16),
+        ],
+        axis=1,
     )
-    mine = jnp.take(pieces, stripe_owner, axis=0)
-    live = jnp.arange(slots, dtype=jnp.int32)[None, :] < counts[0][:, None]
-    asked = jnp.where(live, requests[0] + LEAD, rows_dev + LEAD)
-    asked, mine = lax.optimization_barrier((asked, mine))
+    message = lax.all_to_all(message, AXES, split_axis=0, concat_axis=0, tiled=True)
+    mine = jnp.take(message[:, :piece], stripe_owner, axis=0)
+    mine = jnp.dot(mine, weight, preferred_element_type=jnp.float32).astype(jnp.bfloat16)
     stripes = lax.all_gather(mine[None], AXES, axis=0, tiled=True)
-    wanted = lax.all_to_all(asked, AXES, split_axis=0, concat_axis=0, tiled=True).reshape(-1)
-    selected = gather_rows(wanted, projected, 0, halves, owners)
-    selected, wanted = lax.optimization_barrier((selected, wanted))
+    digits = message[:, piece:].astype(jnp.int32).reshape(owners, 2, slots)
+    wanted = (digits[:, 0] * 128 + digits[:, 1]).reshape(-1)
+    selected = gather_rows(wanted, features, weight, 0, halves, owners, 0, owners)
+    if EARLY:
+        ahead = gather_rows(wanted, features, weight, 1, halves, owners, 0, EARLY)
+        selected, wanted, ahead = lax.optimization_barrier((selected, wanted, ahead))
+    else:
+        ahead = None
+        selected, wanted = lax.optimization_barrier((selected, wanted))
     received = lax.all_to_all(selected, AXES, split_axis=0, concat_axis=0, tiled=True)
-    selected = gather_rows(wanted, projected, 1, halves, owners)
+    selected = gather_rows(wanted, features, weight, 1, halves, owners, EARLY, owners, ahead)
     total = sparse_sum(sparse_rows[0], sparse_cols[0], received, sparse_vals[0], rows_dev, 0, halves)
     received = lax.all_to_all(selected, AXES, split_axis=0, concat_axis=0, tiled=True)
     total = dense_sum(

time: 219 us -> 207 us (0.945)
  blocking collectives: 15.4 us -> 0 us
  other arithmetic: 0.81 us -> 5.63 us
  Pallas kernels: 76 us -> 71.4 us
  waiting for transfers between devices: 84.5 us -> 88.4 us
    all_gather x1, waiting for transfers between devices: 0.02 us -> 18.7 us  [local(): stripes = lax.all_gather(mine[None], AXES, axis=0, tiled=True)]
    all_to_all x2, waiting for transfers between devices: 65.9 us -> 48.4 us  [local(): lax.all_to_all(selected, AXES, split_axis=0, concat_axis=0, tiled=True)]
    all_to_all x1 -> x0, blocking collectives: 15.4 us -> none  [local(): lax.all_to_all(asked, AXES, split_axis=0, concat_axis=0, tiled=True)]
    pallas_call x2 -> x3, Pallas kernels: 37.9 us -> 44.1 us  [gather_rows(): pl.pallas_call(functools.partial(gather_kernel, half=half, halves=halves,...]
    pallas_call x2, Pallas kernels: 22.1 us -> 16.5 us  [sparse_sum(): pl.pallas_call(functools.partial(sparse_kernel, half=half, halves=halves,...]
    pallas_call x1, Pallas kernels: 16 us -> 10.8 us  [dense_sum(): pl.pallas_call(dense_kernel, grid_spec=pltpu.PrefetchScalarGridSpec(num_s...]
    all_to_all x1, waiting for transfers between devices: 18.6 us -> 21.3 us  [local(): lax.all_to_all(message, AXES, split_axis=0, concat_axis=0, tiled=True)]
    concatenate x0 -> x1, other arithmetic: none -> 2.62 us  [local(): jnp.concatenate([features.reshape(owners, piece, width), (asked // 128).a...]
  transfers between devices with their start and end apart: 4 -> 4, of which waited for: 3 -> 4; matrix products, arithmetic and copies ran while one was open for 1% -> 1% of each run, Pallas kernels for 30% -> 31%
where the time goes in v3:
time: 207 us; the launch traced here: 206 us
  waiting for transfers between devices  88.4 us (43%)
  Pallas kernels  71.4 us (34%)
  starting transfers between devices  24 us (12%)
  between operations  13.6 us (7%)
  other arithmetic  5.63 us (3%)
  local copies, waits for them, and re-layouts  2.2 us (1%)
    all_to_all x2, waiting for transfers between devices, local(): lax.all_to_all(selected, AXES, split_axis=0, concat_axis=0, tiled=True)  48.4 us
    pallas_call x3, Pallas kernels, gather_rows(): pl.pallas_call(functools.partial(gather_kernel, half=half, halves=halves,...  44.1 us
    all_to_all x1, waiting for transfers between devices, local(): lax.all_to_all(message, AXES, split_axis=0, concat_axis=0, tiled=True)  21.3 us
    all_gather x1, waiting for transfers between devices, local(): stripes = lax.all_gather(mine[None], AXES, axis=0, tiled=True)  18.7 us
    pallas_call x2, Pallas kernels, sparse_sum(): pl.pallas_call(functools.partial(sparse_kernel, half=half, halves=halves,...  16.5 us
    all_to_all x2, starting transfers between devices, local(): lax.all_to_all(selected, AXES, split_axis=0, concat_axis=0, tiled=True)  12.4 us
    all_to_all x1, starting transfers between devices, local(): lax.all_to_all(message, AXES, split_axis=0, concat_axis=0, tiled=True)  11.5 us
    pallas_call x1, Pallas kernels, dense_sum(): pl.pallas_call(dense_kernel, grid_spec=pltpu.PrefetchScalarGridSpec(num_s...  10.8 us
  transfers between devices with their start and end apart: 4, of which 4 were waited for; matrix products, arithmetic and copies ran while one was open for 1% of the time, Pallas kernels for 31%

profile of v3, /device:TPU:1, one launch (start us, length us, event | category | flops | bytes accessed | tf_op | source)
XLA Modules:
  0.0 206.0 jit_solution(3831727296926290534)
XLA Ops:
  6.5 0.9 broadcast_add_fusion
  7.5 0.1 add.34
  7.5 1.1 fusion.1
  8.6 0.0 copy-start.3
  8.6 0.1 fusion
  8.8 2.6 %pad_maximum_fusion = bf16[128,36,128]{2,1,0:T(8,128)(2,1)} fusion(bf16[128,2,128]{2,1,0:T(2,128)(2,1)S(1)} %fusion, bf16[128,2,128]{2,1,0:T(2,128)(2,1)S(1)} %get-tuple-element.11, bf16[128,32,128]{2,1,0:T(8,128)(2,1)} %bitcast.13), kind=kLoop, calls=%fused_computation.1 | loop fusion | flops 3538944 | bytes 2359296 | tf_op jit(solution)/shard_map/concatenate | solution.py:236
  11.4 0.0 copy-start
  11.4 11.5 %all-to-all-start = ((bf16[128,36,128]{2,1,0:T(8,128)(2,1)}), bf16[128,36,128]{2,1,0:T(8,128)(2,1)S(1)}, u32[]{:S(2)}, u32[]{:S(2)}) async-start(bf16[128,36,128]{2,1,0:T(8,128)(2,1)} %pad_maximum_fusion), calls=%async_computation | async-start | bytes 2621440 | tf_op jit(solution)/shard_map/all_to_all | solution.py:244
  22.9 0.0 all-gather.3.cloned.1.call-start
  22.9 0.0 copy-done.3
  23.0 21.3 %all-to-all-done = bf16[128,36,128]{2,1,0:T(8,128)(2,1)S(1)} async-done(((bf16[128,36,128]{2,1,0:T(8,128)(2,1)}), bf16[128,36,128]{2,1,0:T(8,128)(2,1)S(1)}, u32[]{:S(2)}, u32[]{:S(2)}) %all-to-all-start) | async-done | bytes 1179680 | tf_op jit(solution)/shard_map/all_to_all | solution.py:244
  44.3 0.1 slice.21
  44.3 0.6 gather_fusion
  44.9 0.0 copy-done
  44.9 0.8 convolution_convert_fusion
  45.8 0.0 all-gather.3.cloned.1.call-update
  45.8 0.1 slice_convert_fusion
  45.8 0.2 reshape.55
  46.1 0.8 slice_add_fusion
  46.9 19.3 %gather_rows.3 = bf16[128,128,128]{2,1,0:T(8,128)(2,1)} custom-call(s32[32768]{0:T(1024)} %bitcast.16, bf16[4096,128]{1,0:T(8,128)(2,1)} %features_ref.5, bf16[128,128]{1,0:T(8,128)(2,1)} %weight_ref.5), custom_call_target="tpu_custom_call" | custom-call | tf_op jit(solution)/shard_map/gather_rows/pallas_call | solution.py:54
  66.2 7.8 %gather_rows.4.refs_0_ = bf16[128,128,128]{2,1,0:T(8,128)(2,1)} custom-call(s32[32768]{0:T(1024)} %bitcast.17, bf16[4096,128]{1,0:T(8,128)(2,1)} %features_ref.5, bf16[128,128]{1,0:T(8,128)(2,1)} %weight_ref.5), custom_call_target="tpu_custom_call" | custom-call | tf_op jit(solution)/shard_map/gather_rows/pallas_call | solution.py:54
  74.1 6.0 %all-to-all-start.2 = ((bf16[128,128,128]{2,1,0:T(8,128)(2,1)}), bf16[128,128,128]{2,1,0:T(8,128)(2,1)}, u32[]{:S(2)}, u32[]{:S(2)}) async-start(bf16[128,128,128]{2,1,0:T(8,128)(2,1)} %gather_rows.3), calls=%async_computation.2 | async-start | bytes 8388608 | tf_op jit(solution)/shard_map/all_to_all | solution.py:257
  80.1 17.0 %gather_rows.5 = bf16[128,128,128]{2,1,0:T(8,128)(2,1)} custom-call(s32[32768]{0:T(1024)} %bitcast.18, bf16[4096,128]{1,0:T(8,128)(2,1)} %features_ref.5, bf16[128,128]{1,0:T(8,128)(2,1)} %weight_ref.5, bf16[128,128,128]{2,1,0:T(8,128)(2,1)} %gather_rows.4.refs_0_), custom_call_target="tpu_custom_call", output_to_operand_aliasing={{}: (3, {})} | custom-call | tf_op jit(solution)/shard_map/gather_rows/pallas_call | solution.py:54
  97.0 0.0 copy-start.1
  97.0 0.0 copy-start.2
  97.0 35.5 %all-to-all-done.2.source_hbm = bf16[128,128,128]{2,1,0:T(8,128)(2,1)} async-done(((bf16[128,128,128]{2,1,0:T(8,128)(2,1)}), bf16[128,128,128]{2,1,0:T(8,128)(2,1)}, u32[]{:S(2)}, u32[]{:S(2)}) %all-to-all-start.2) | async-done | bytes 4194336 | tf_op jit(solution)/shard_map/all_to_all | solution.py:257
  132.6 6.4 %all-to-all-start.1 = ((bf16[128,128,128]{2,1,0:T(8,128)(2,1)}), bf16[128,128,128]{2,1,0:T(8,128)(2,1)}, u32[]{:S(2)}, u32[]{:S(2)}) async-start(bf16[128,128,128]{2,1,0:T(8,128)(2,1)} %gather_rows.5), calls=%async_computation.1 | async-start | bytes 8388608 | tf_op jit(solution)/shard_map/all_to_all | solution.py:260
  139.0 0.0 copy-done.1
  139.0 0.6 reshape.51.rows_ref
  139.7 0.0 copy-done.2
  139.7 0.6 reshape.52.cols_ref
  140.3 8.4 %sparse_sum.2.begin_hbm = f32[4096,128]{1,0:T(8,128)} custom-call(s32[256]{0:T(256)} %bitcast.19, s32[256]{0:T(256)} %bitcast.21, bf16[128,128,128]{2,1,0:T(8,128)(2,1)} %all-to-all-done.2.source_hbm, bf16[256,128,128]{2,1,0:T(8,128)(2,1)} %bitcast.11), custom_call_target="tpu_custom_call" | custom-call | tf_op jit(solution)/shard_map/sparse_sum/pallas_call | solution.py:192
  148.7 18.7 %all-gather.3.cloned.1.call-done = bf16[1024,32,128]{2,1,0:T(8,128)(2,1)} async-done(((bf16[8,32,128]{2,1,0:T(8,128)(2,1)}), bf16[1024,32,128]{2,1,0:T(8,128)(2,1)}) %all-gather.3.cloned.1.call-update) | async-done | bytes 8388624 | tf_op jit(solution)/shard_map/all_gather | solution.py:247
  167.4 10.8 %dense_sum.1.refs_0_ = f32[4096,128]{1,0:T(8,128)} custom-call(s32[256]{0:T(256)} %reshape.51.rows_ref, s32[256]{0:T(256)} %reshape.52.cols_ref, bf16[128,8,32,128]{3,2,1,0:T(8,128)(2,1)} %bitcast.15, bf16[256,128,128]{2,1,0:T(8,128)(2,1)} %bitcast.14, f32[4096,128]{1,0:T(8,128)} %sparse_sum.2.begin_hbm), custom_call_target="tpu_custom_call" | custom-call | tf_op jit(solution)/shard_map/dense_sum/pallas_call | solution.py:117
  178.2 12.9 %all-to-all-done.1.source_hbm = bf16[128,128,128]{2,1,0:T(8,128)(2,1)} async-done(((bf16[128,128,128]{2,1,0:T(8,128)(2,1)}), bf16[128,128,128]{2,1,0:T(8,128)(2,1)}, u32[]{:S(2)}, u32[]{:S(2)}) %all-to-all-start.1) | async-done | bytes 4194336 | tf_op jit(solution)/shard_map/all_to_all | solution.py:260
  191.1 8.1 %sparse_sum.3 = bf16[4096,128]{1,0:T(8,128)(2,1)} custom-call(s32[256]{0:T(256)} %bitcast.20, s32[256]{0:T(256)} %bitcast.22, bf16[128,128,128]{2,1,0:T(8,128)(2,1)} %all-to-all-done.1.source_hbm, bf16[256,128,128]{2,1,0:T(8,128)(2,1)} %bitcast.12, f32[4096,128]{1,0:T(8,128)} %dense_sum.1.refs_0_), custom_call_target="tpu_custom_call" | custom-call | tf_op jit(solution)/shard_map/sparse_sum/pallas_call | solution.py:192
  (4 shorter events, 0.0 us)
Async XLA Ops:
  8.6 14.3 %copy-start.3 = (s32[8]{0:T(128)S(1)}, s32[8]{0:T(128)}, u32[]{:S(2)}) copy-start(s32[8]{0:T(128)} %param.13) | copy-start | bytes 100
  11.4 33.5 %copy-start = (bf16[128,128]{1,0:T(8,128)(2,1)S(1)}, bf16[128,128]{1,0:T(8,128)(2,1)}, u32[]{:S(2)}) copy-start(bf16[128,128]{1,0:T(8,128)(2,1)} %weight_ref.5) | copy-start | bytes 98308
  11.4 32.9 %all-to-all-start = ((bf16[128,36,128]{2,1,0:T(8,128)(2,1)}), bf16[128,36,128]{2,1,0:T(8,128)(2,1)S(1)}, u32[]{:S(2)}, u32[]{:S(2)}) async-start(bf16[128,36,128]{2,1,0:T(8,128)(2,1)} %pad_maximum_fusion), calls=%async_computation | async-start | bytes 2621440 | tf_op jit(solution)/shard_map/all_to_all | solution.py:244
  22.9 144.5 %all-gather.3.cloned.1.call-start = ((), (), s32[]{:S(2)}) async-start(), calls=%async_computation.3 | async-start | bytes 8454144 | tf_op jit(solution)/shard_map/all_gather | solution.py:247
  74.1 58.5 %all-to-all-start.2 = ((bf16[128,128,128]{2,1,0:T(8,128)(2,1)}), bf16[128,128,128]{2,1,0:T(8,128)(2,1)}, u32[]{:S(2)}, u32[]{:S(2)}) async-start(bf16[128,128,128]{2,1,0:T(8,128)(2,1)} %gather_rows.3), calls=%async_computation.2 | async-start | bytes 8388608 | tf_op jit(solution)/shard_map/all_to_all | solution.py:257
  97.0 42.0 %copy-start.1 = (s32[1,8,32]{2,1,0:T(8,128)S(1)}, s32[1,8,32]{2,1,0:T(8,128)}, u32[]{:S(2)}) copy-start(s32[1,8,32]{2,1,0:T(8,128)} %param.15) | copy-start | bytes 3076
  97.0 42.6 %copy-start.2 = (s32[1,8,32]{2,1,0:T(8,128)S(1)}, s32[1,8,32]{2,1,0:T(8,128)}, u32[]{:S(2)}) copy-start(s32[1,8,32]{2,1,0:T(8,128)} %param.16) | copy-start | bytes 3076
  132.6 58.5 %all-to-all-start.1 = ((bf16[128,128,128]{2,1,0:T(8,128)(2,1)}), bf16[128,128,128]{2,1,0:T(8,128)(2,1)}, u32[]{:S(2)}, u32[]{:S(2)}) async-start(bf16[128,128,128]{2,1,0:T(8,128)(2,1)} %gather_rows.5), calls=%async_computation.1 | async-start | bytes 8388608 | tf_op jit(solution)/shard_map/all_to_all | solution.py:260
Sparse Core Ops, SparseCore 0:
  45.9 121.4 all-gather.2

commit v4 on v3

--- a/solution.py
+++ b/solution.py
@@ -13,6 +13,32 @@
 UNROLL = 32
 LOADS = 4
 EARLY = 24
+
+
+def message_kernel(features_ref, requests_ref, counts_ref, out_ref, *, nodes):
+    owners, slots = requests_ref.shape
+    width = features_ref.shape[2]
+    live = jnp.broadcast_to(counts_ref[...], (owners, owners)).T
+    lane = lax.broadcasted_iota(jnp.int32, (owners, width), 1)
+    rows = []
+    for half in range(slots // width):
+        at = pl.ds(half * width, width)
+        rows.append(jnp.where(lane + half * width < live, requests_ref[:, at] + LEAD, nodes + LEAD))
+    digits = [row // width for row in rows] + [row % width for row in rows]
+    digits = jnp.stack([digit.astype(jnp.float32) for digit in digits], axis=1)
+    out_ref[...] = jnp.concatenate([features_ref[...], digits.astype(jnp.bfloat16)], axis=1)
+
+
+def build_message(features, requests, counts, owners):
+    nodes, width = features.shape
+    piece = nodes // owners
+    rows = piece + 2 * requests.shape[1] // width
+    return pl.pallas_call(
+        functools.partial(message_kernel, nodes=nodes),
+        out_shape=jax.ShapeDtypeStruct((owners, rows, width), jnp.bfloat16),
+        compiler_params=pltpu.CompilerParams(vmem_limit_bytes=VMEM),
+        name="build_message",
+    )(features.reshape(owners, piece, width), requests, counts)
 
 
 def gather_kernel(index_ref, features_ref, weight_ref, *refs, half, halves, first_owner):
@@ -231,16 +257,7 @@
     slots = requests.shape[2]
     halves = slots // tile
     piece = rows_dev // owners
-    live = jnp.arange(slots, dtype=jnp.int32)[None, :] < counts[0][:, None]
-    asked = jnp.where(live, requests[0] + LEAD, rows_dev + LEAD).reshape(owners, halves, tile)
-    message = jnp.concatenate(
-        [
-            features.reshape(owners, piece, width),
-            (asked // 128).astype(jnp.bfloat16),
-            (asked % 128).astype(jnp.bfloat16),
-        ],
-        axis=1,
-    )
+    message = build_message(features, requests[0], counts, owners)
     message = lax.all_to_all(message, AXES, split_axis=0, concat_axis=0, tiled=True)
     mine = jnp.take(message[:, :piece], stripe_owner, axis=0)
     mine = jnp.dot(mine, weight, preferred_element_type=jnp.float32).astype(jnp.bfloat16)

time: 207 us -> 205 us (level)
  other arithmetic: 5.63 us -> 0.89 us
  Pallas kernels: 71.4 us -> 74.5 us
    pallas_call x0 -> x1, Pallas kernels: none -> 3.11 us  [build_message(): pl.pallas_call(functools.partial(message_kernel, nodes=nodes), out_shape=...]
    concatenate x1 -> x0, other arithmetic: 2.62 us -> none  [local(): jnp.concatenate([features.reshape(owners, piece, width), (asked // 128).a...]
where the time goes in v4:
time: 205 us; the launch traced here: 204 us
  waiting for transfers between devices  88.5 us (43%)
  Pallas kernels  74.5 us (36%)
  starting transfers between devices  23.9 us (12%)
  between operations  13.5 us (7%)
  local copies, waits for them, and re-layouts  2.17 us (1%)
    all_to_all x2, waiting for transfers between devices, local(): lax.all_to_all(selected, AXES, split_axis=0, concat_axis=0, tiled=True)  48.5 us
    pallas_call x3, Pallas kernels, gather_rows(): pl.pallas_call(functools.partial(gather_kernel, half=half, halves=halves,...  44.1 us
    all_to_all x1, waiting for transfers between devices, local(): lax.all_to_all(message, AXES, split_axis=0, concat_axis=0, tiled=True)  21.3 us
    all_gather x1, waiting for transfers between devices, local(): stripes = lax.all_gather(mine[None], AXES, axis=0, tiled=True)  18.7 us
    pallas_call x2, Pallas kernels, sparse_sum(): pl.pallas_call(functools.partial(sparse_kernel, half=half, halves=halves,...  16.5 us
    all_to_all x2, starting transfers between devices, local(): lax.all_to_all(selected, AXES, split_axis=0, concat_axis=0, tiled=True)  12.4 us
    all_to_all x1, starting transfers between devices, local(): lax.all_to_all(message, AXES, split_axis=0, concat_axis=0, tiled=True)  11.5 us
    pallas_call x1, Pallas kernels, dense_sum(): pl.pallas_call(dense_kernel, grid_spec=pltpu.PrefetchScalarGridSpec(num_s...  10.8 us
  transfers between devices with their start and end apart: 4, of which 4 were waited for; matrix products, arithmetic and copies ran while one was open for 1% of the time, Pallas kernels for 31%

profile of v4, /device:TPU:1, one launch (start us, length us, event | category | flops | bytes accessed | tf_op | source)
XLA Modules:
  0.0 204.3 jit_solution(16972031420583149616)
XLA Ops:
  6.5 0.0 copy-start.3
  6.5 0.0 copy-start
  6.5 3.1 %build_message.1 = bf16[128,36,128]{2,1,0:T(8,128)(2,1)} custom-call(bf16[128,32,128]{2,1,0:T(8,128)(2,1)} %bitcast.13, s32[128,256]{1,0:T(8,128)} %bitcast.19, s32[1,128]{1,0:T(1,128)} %counts_ref.1), custom_call_target="tpu_custom_call" | custom-call | tf_op jit(solution)/shard_map/build_message/pallas_call | solution.py:36
  9.7 11.5 %all-to-all-start = ((bf16[128,36,128]{2,1,0:T(8,128)(2,1)}), bf16[128,36,128]{2,1,0:T(8,128)(2,1)S(1)}, u32[]{:S(2)}, u32[]{:S(2)}) async-start(bf16[128,36,128]{2,1,0:T(8,128)(2,1)} %build_message.1), calls=%async_computation | async-start | bytes 2621440 | tf_op jit(solution)/shard_map/all_to_all | solution.py:261
  21.2 0.0 all-gather.3.cloned.1.call-start
  21.2 0.0 copy-done.3
  21.3 21.3 %all-to-all-done = bf16[128,36,128]{2,1,0:T(8,128)(2,1)S(1)} async-done(((bf16[128,36,128]{2,1,0:T(8,128)(2,1)}), bf16[128,36,128]{2,1,0:T(8,128)(2,1)S(1)}, u32[]{:S(2)}, u32[]{:S(2)}) %all-to-all-start) | async-done | bytes 1179680 | tf_op jit(solution)/shard_map/all_to_all | solution.py:261
  42.5 0.1 slice.21
  42.6 0.6 gather_fusion
  43.2 0.0 copy-done
  43.2 0.8 convolution_convert_fusion
  44.0 0.0 all-gather.3.cloned.1.call-update
  44.1 0.1 slice_convert_fusion
  44.1 0.2 reshape.36
  44.3 0.8 slice_add_fusion
  45.2 19.3 %gather_rows.3 = bf16[128,128,128]{2,1,0:T(8,128)(2,1)} custom-call(s32[32768]{0:T(1024)} %bitcast.16, bf16[4096,128]{1,0:T(8,128)(2,1)} %features_ref.5, bf16[128,128]{1,0:T(8,128)(2,1)} %weight_ref.5), custom_call_target="tpu_custom_call" | custom-call | tf_op jit(solution)/shard_map/gather_rows/pallas_call | solution.py:80
  64.5 7.8 %gather_rows.4.refs_0_ = bf16[128,128,128]{2,1,0:T(8,128)(2,1)} custom-call(s32[32768]{0:T(1024)} %bitcast.17, bf16[4096,128]{1,0:T(8,128)(2,1)} %features_ref.5, bf16[128,128]{1,0:T(8,128)(2,1)} %weight_ref.5), custom_call_target="tpu_custom_call" | custom-call | tf_op jit(solution)/shard_map/gather_rows/pallas_call | solution.py:80
  72.3 6.0 %all-to-all-start.2 = ((bf16[128,128,128]{2,1,0:T(8,128)(2,1)}), bf16[128,128,128]{2,1,0:T(8,128)(2,1)}, u32[]{:S(2)}, u32[]{:S(2)}) async-start(bf16[128,128,128]{2,1,0:T(8,128)(2,1)} %gather_rows.3), calls=%async_computation.2 | async-start | bytes 8388608 | tf_op jit(solution)/shard_map/all_to_all | solution.py:274
  78.3 17.0 %gather_rows.5 = bf16[128,128,128]{2,1,0:T(8,128)(2,1)} custom-call(s32[32768]{0:T(1024)} %bitcast.18, bf16[4096,128]{1,0:T(8,128)(2,1)} %features_ref.5, bf16[128,128]{1,0:T(8,128)(2,1)} %weight_ref.5, bf16[128,128,128]{2,1,0:T(8,128)(2,1)} %gather_rows.4.refs_0_), custom_call_target="tpu_custom_call", output_to_operand_aliasing={{}: (3, {})} | custom-call | tf_op jit(solution)/shard_map/gather_rows/pallas_call | solution.py:80
  95.3 0.0 copy-start.1
  95.3 0.0 copy-start.2
  95.3 35.6 %all-to-all-done.2.source_hbm = bf16[128,128,128]{2,1,0:T(8,128)(2,1)} async-done(((bf16[128,128,128]{2,1,0:T(8,128)(2,1)}), bf16[128,128,128]{2,1,0:T(8,128)(2,1)}, u32[]{:S(2)}, u32[]{:S(2)}) %all-to-all-start.2) | async-done | bytes 4194336 | tf_op jit(solution)/shard_map/all_to_all | solution.py:274
  130.8 6.3 %all-to-all-start.1 = ((bf16[128,128,128]{2,1,0:T(8,128)(2,1)}), bf16[128,128,128]{2,1,0:T(8,128)(2,1)}, u32[]{:S(2)}, u32[]{:S(2)}) async-start(bf16[128,128,128]{2,1,0:T(8,128)(2,1)} %gather_rows.5), calls=%async_computation.1 | async-start | bytes 8388608 | tf_op jit(solution)/shard_map/all_to_all | solution.py:277
  137.2 0.0 copy-done.1
  137.2 0.6 reshape.32.rows_ref
  137.9 0.0 copy-done.2
  137.9 0.7 reshape.33.cols_ref
  138.5 8.4 %sparse_sum.2.begin_hbm = f32[4096,128]{1,0:T(8,128)} custom-call(s32[256]{0:T(256)} %bitcast.20, s32[256]{0:T(256)} %bitcast.22, bf16[128,128,128]{2,1,0:T(8,128)(2,1)} %all-to-all-done.2.source_hbm, bf16[256,128,128]{2,1,0:T(8,128)(2,1)} %bitcast.11), custom_call_target="tpu_custom_call" | custom-call | tf_op jit(solution)/shard_map/sparse_sum/pallas_call | solution.py:218
  146.9 18.7 %all-gather.3.cloned.1.call-done = bf16[1024,32,128]{2,1,0:T(8,128)(2,1)} async-done(((bf16[8,32,128]{2,1,0:T(8,128)(2,1)}), bf16[1024,32,128]{2,1,0:T(8,128)(2,1)}) %all-gather.3.cloned.1.call-update) | async-done | bytes 8388624 | tf_op jit(solution)/shard_map/all_gather | solution.py:264
  165.6 10.8 %dense_sum.1.refs_0_ = f32[4096,128]{1,0:T(8,128)} custom-call(s32[256]{0:T(256)} %reshape.32.rows_ref, s32[256]{0:T(256)} %reshape.33.cols_ref, bf16[128,8,32,128]{3,2,1,0:T(8,128)(2,1)} %bitcast.15, bf16[256,128,128]{2,1,0:T(8,128)(2,1)} %bitcast.14, f32[4096,128]{1,0:T(8,128)} %sparse_sum.2.begin_hbm), custom_call_target="tpu_custom_call" | custom-call | tf_op jit(solution)/shard_map/dense_sum/pallas_call | solution.py:143
  176.4 13.0 %all-to-all-done.1.source_hbm = bf16[128,128,128]{2,1,0:T(8,128)(2,1)} async-done(((bf16[128,128,128]{2,1,0:T(8,128)(2,1)}), bf16[128,128,128]{2,1,0:T(8,128)(2,1)}, u32[]{:S(2)}, u32[]{:S(2)}) %all-to-all-start.1) | async-done | bytes 4194336 | tf_op jit(solution)/shard_map/all_to_all | solution.py:277
  189.4 8.1 %sparse_sum.3 = bf16[4096,128]{1,0:T(8,128)(2,1)} custom-call(s32[256]{0:T(256)} %bitcast.21, s32[256]{0:T(256)} %bitcast.23, bf16[128,128,128]{2,1,0:T(8,128)(2,1)} %all-to-all-done.1.source_hbm, bf16[256,128,128]{2,1,0:T(8,128)(2,1)} %bitcast.12, f32[4096,128]{1,0:T(8,128)} %dense_sum.1.refs_0_), custom_call_target="tpu_custom_call" | custom-call | tf_op jit(solution)/shard_map/sparse_sum/pallas_call | solution.py:218
  (3 shorter events, 0.0 us)
Async XLA Ops:
  6.5 14.7 %copy-start.3 = (s32[8]{0:T(128)S(1)}, s32[8]{0:T(128)}, u32[]{:S(2)}) copy-start(s32[8]{0:T(128)} %param.13) | copy-start | bytes 100
  6.5 36.6 %copy-start = (bf16[128,128]{1,0:T(8,128)(2,1)S(1)}, bf16[128,128]{1,0:T(8,128)(2,1)}, u32[]{:S(2)}) copy-start(bf16[128,128]{1,0:T(8,128)(2,1)} %weight_ref.5) | copy-start | bytes 98308
  9.7 32.9 %all-to-all-start = ((bf16[128,36,128]{2,1,0:T(8,128)(2,1)}), bf16[128,36,128]{2,1,0:T(8,128)(2,1)S(1)}, u32[]{:S(2)}, u32[]{:S(2)}) async-start(bf16[128,36,128]{2,1,0:T(8,128)(2,1)} %build_message.1), calls=%async_computation | async-start | bytes 2621440 | tf_op jit(solution)/shard_map/all_to_all | solution.py:261
  21.2 144.4 %all-gather.3.cloned.1.call-start = ((), (), s32[]{:S(2)}) async-start(), calls=%async_computation.3 | async-start | bytes 8454144 | tf_op jit(solution)/shard_map/all_gather | solution.py:264
  72.3 58.5 %all-to-all-start.2 = ((bf16[128,128,128]{2,1,0:T(8,128)(2,1)}), bf16[128,128,128]{2,1,0:T(8,128)(2,1)}, u32[]{:S(2)}, u32[]{:S(2)}) async-start(bf16[128,128,128]{2,1,0:T(8,128)(2,1)} %gather_rows.3), calls=%async_computation.2 | async-start | bytes 8388608 | tf_op jit(solution)/shard_map/all_to_all | solution.py:274
  95.3 41.9 %copy-start.1 = (s32[1,8,32]{2,1,0:T(8,128)S(1)}, s32[1,8,32]{2,1,0:T(8,128)}, u32[]{:S(2)}) copy-start(s32[1,8,32]{2,1,0:T(8,128)} %param.15) | copy-start | bytes 3076
  95.3 42.6 %copy-start.2 = (s32[1,8,32]{2,1,0:T(8,128)S(1)}, s32[1,8,32]{2,1,0:T(8,128)}, u32[]{:S(2)}) copy-start(s32[1,8,32]{2,1,0:T(8,128)} %param.16) | copy-start | bytes 3076
  130.8 58.5 %all-to-all-start.1 = ((bf16[128,128,128]{2,1,0:T(8,128)(2,1)}), bf16[128,128,128]{2,1,0:T(8,128)(2,1)}, u32[]{:S(2)}, u32[]{:S(2)}) async-start(bf16[128,128,128]{2,1,0:T(8,128)(2,1)} %gather_rows.5), calls=%async_computation.1 | async-start | bytes 8388608 | tf_op jit(solution)/shard_map/all_to_all | solution.py:277
Sparse Core Ops, SparseCore 0:
  44.2 121.3 all-gather.2

commit v5 on v4

--- a/solution.py
+++ b/solution.py
@@ -10,9 +10,14 @@
 AXES = ("gx", "gy")
 LEAD = 8
 VMEM = 56 * 1024 * 1024
+VMEM_TILES = 36 * 1024 * 1024
 UNROLL = 32
 LOADS = 4
-EARLY = 24
+EARLY = 32
+
+
+def in_hbm(array):
+    return pltpu.with_memory_space_constraint(array, pltpu.HBM)
 
 
 def message_kernel(features_ref, requests_ref, counts_ref, out_ref, *, nodes):
@@ -156,86 +161,144 @@
             ],
         ),
         out_shape=jax.ShapeDtypeStruct(begin.shape, jnp.float32),
-        compiler_params=pltpu.CompilerParams(vmem_limit_bytes=VMEM),
+        compiler_params=pltpu.CompilerParams(vmem_limit_bytes=VMEM_TILES),
         name="dense_sum",
-    )(rows, cols, source, values, begin)
-
-
-def sparse_kernel(rows_ref, cols_ref, source_hbm, values_ref, *refs, half, halves, last):
-    out_ref, source_ref, held_ref, total_ref, begin_ref, list_ref, sems, value_sems = refs[-8:]
+    )(rows, cols, in_hbm(source), in_hbm(values), in_hbm(begin))
+
+
+def choose_half(cols_ref, list_ref, count, half, halves):
+    def choose(k, taken):
+        list_ref[taken] = k
+        return taken + jnp.where(cols_ref[k] % halves == half, 1, 0)
+
+    return lax.fori_loop(0, count, choose, 0, unroll=8)
+
+
+def first_kernel(
+    rows_ref, cols_ref, source_hbm, values_ref, out_ref, picked_ref, later_ref, source_ref, held_ref, total_ref, list_ref,
+    source_sem, value_sems,
+):
     nodes = out_ref.shape[0]
     count = held_ref.shape[0]
-    load_source = pltpu.make_async_copy(source_hbm, source_ref, sems.at[0])
+    load_source = pltpu.make_async_copy(source_hbm, source_ref, source_sem)
     load_source.start()
     for part in range(LOADS):
         value_copy(values_ref, held_ref, value_sems, part).start()
-    if last:
-        load_begin = pltpu.make_async_copy(refs[0], begin_ref, sems.at[1])
-        load_begin.start()
     total_ref[...] = jnp.zeros_like(total_ref)
-
-    def choose(k, taken):
-        list_ref[taken] = k
-        return taken + jnp.where(cols_ref[k] % halves == half, 1, 0)
-
-    taken = lax.fori_loop(0, count, choose, 0, unroll=8)
+    taken = choose_half(cols_ref, list_ref, count, 0, 2)
+    later = choose_half(cols_ref, later_ref, count, 1, 2)
+    later_ref[count] = later
     load_source.wait()
-    size = count // LOADS
-
-    def wait_part(part, carry):
+    for part in range(LOADS):
         value_copy(values_ref, held_ref, value_sems, part).wait()
-        return carry
-
-    def group(step, ready):
-        last_k = list_ref[jnp.minimum(step * UNROLL + UNROLL, taken) - 1]
-        need = last_k // size + 1
-        lax.fori_loop(ready, need, wait_part, 0)
+
+    def group(step, carry):
         for j in range(UNROLL):
             entry = step * UNROLL + j
-            real = entry < taken
-            k = jnp.where(real, list_ref[jnp.minimum(entry, taken - 1)], last_k)
-            row = jnp.where(real, rows_ref[k], nodes // 128)
-            block = source_ref[cols_ref[k] // halves]
-            product = jnp.dot(held_ref[k], block, preferred_element_type=jnp.float32)
+            k = list_ref[jnp.minimum(entry, taken - 1)]
+            row = jnp.where(entry < taken, rows_ref[k], nodes // 128)
+            product = jnp.dot(held_ref[k], source_ref[cols_ref[k] // 2], preferred_element_type=jnp.float32)
             at = pl.ds(pl.multiple_of(row * 128, 128), 128)
             total_ref[at, :] += product
-        return jnp.maximum(ready, need)
-
-    ready = lax.fori_loop(0, pl.cdiv(taken, UNROLL), group, 0)
-    lax.fori_loop(ready, LOADS, wait_part, 0)
-    result = total_ref[pl.ds(0, nodes), :]
-    if last:
-        load_begin.wait()
-        result = jnp.maximum(result + begin_ref[...], 0.0)
-    out_ref[...] = result.astype(out_ref.dtype)
-
-
-def sparse_sum(rows, cols, source, values, nodes, half, halves, begin=None):
+        return carry
+
+    lax.fori_loop(0, pl.cdiv(taken, UNROLL), group, 0)
+
+    def pick(entry, carry):
+        picked_ref[entry] = held_ref[later_ref[entry]]
+        return carry
+
+    lax.fori_loop(0, later, pick, 0)
+    out_ref[...] = total_ref[pl.ds(0, nodes), :]
+
+
+def first_sum(rows, cols, source, values, nodes):
     hbm = pl.BlockSpec(memory_space=pl.ANY)
     shape = (nodes, source.shape[-1])
-    last = begin is not None
-    more = [begin] if last else []
-    return pl.pallas_call(
-        functools.partial(sparse_kernel, half=half, halves=halves, last=last),
+    count = values.shape[0]
+    return pl.pallas_call(
+        first_kernel,
         grid_spec=pltpu.PrefetchScalarGridSpec(
             num_scalar_prefetch=2,
             grid=(1,),
-            in_specs=[hbm] * (2 + len(more)),
-            out_specs=pl.BlockSpec(shape, lambda i, r, c: (0, 0)),
+            in_specs=[hbm] * 2,
+            out_specs=[
+                pl.BlockSpec(shape, lambda i, r, c: (0, 0)),
+                pl.BlockSpec(values.shape, lambda i, r, c: (0, 0, 0)),
+                pl.BlockSpec(memory_space=pltpu.SMEM),
+            ],
             scratch_shapes=[
                 pltpu.VMEM(source.shape, jnp.bfloat16),
                 pltpu.VMEM(values.shape, jnp.bfloat16),
                 pltpu.VMEM((nodes + 128, shape[1]), jnp.float32),
-                pltpu.VMEM(shape if last else (8, shape[1]), jnp.float32),
-                pltpu.SMEM((values.shape[0] + 8,), jnp.int32),
-                pltpu.SemaphoreType.DMA((2,)),
+                pltpu.SMEM((count + 8,), jnp.int32),
+                pltpu.SemaphoreType.DMA,
                 pltpu.SemaphoreType.DMA((LOADS,)),
             ],
         ),
-        out_shape=jax.ShapeDtypeStruct(shape, jnp.bfloat16 if last else jnp.float32),
-        compiler_params=pltpu.CompilerParams(vmem_limit_bytes=VMEM),
-        name="sparse_sum",
-    )(rows, cols, source, values, *more)
+        out_shape=[
+            jax.ShapeDtypeStruct(shape, jnp.float32),
+            jax.ShapeDtypeStruct(values.shape, jnp.bfloat16),
+            jax.ShapeDtypeStruct((count + 8,), jnp.int32),
+        ],
+        compiler_params=pltpu.CompilerParams(vmem_limit_bytes=VMEM_TILES),
+        name="first_sum",
+    )(rows, cols, in_hbm(source), in_hbm(values))
+
+
+def last_kernel(
+    rows_ref, cols_ref, list_ref, source_ref, begin_ref, values_ref, out_ref, held_ref, total_ref, value_sems
+):
+    nodes = begin_ref.shape[0]
+    count = held_ref.shape[0]
+    taken = list_ref[count]
+
+    def load_values(part):
+        at = pl.ds(part * UNROLL, UNROLL)
+        return pltpu.make_async_copy(values_ref.at[at], held_ref.at[at], value_sems.at[part])
+
+    for part in range(count // UNROLL):
+
+        @pl.when(part * UNROLL < taken)
+        def _():
+            load_values(part).start()
+
+    total_ref[pl.ds(0, nodes), :] = begin_ref[...]
+    total_ref[pl.ds(nodes, 128), :] = jnp.zeros((128, total_ref.shape[1]), jnp.float32)
+
+    def group(step, carry):
+        load_values(step).wait()
+        for j in range(UNROLL):
+            entry = jnp.minimum(step * UNROLL + j, taken - 1)
+            k = list_ref[entry]
+            row = jnp.where(step * UNROLL + j < taken, rows_ref[k], nodes // 128)
+            product = jnp.dot(held_ref[entry], source_ref[cols_ref[k] // 2], preferred_element_type=jnp.float32)
+            at = pl.ds(pl.multiple_of(row * 128, 128), 128)
+            total_ref[at, :] += product
+        return carry
+
+    lax.fori_loop(0, pl.cdiv(taken, UNROLL), group, 0)
+    out_ref[...] = jnp.maximum(total_ref[pl.ds(0, nodes), :], 0.0).astype(jnp.bfloat16)
+
+
+def last_sum(rows, cols, listed, source, values, begin):
+    nodes, width = begin.shape
+    smem = pl.BlockSpec(memory_space=pltpu.SMEM)
+    vmem = pl.BlockSpec(memory_space=pltpu.VMEM)
+    source, begin = (pltpu.with_memory_space_constraint(a, pltpu.VMEM) for a in (source, begin))
+    return pl.pallas_call(
+        last_kernel,
+        in_specs=[smem] * 3 + [vmem] * 2 + [pl.BlockSpec(memory_space=pltpu.HBM)],
+        out_specs=vmem,
+        scratch_shapes=[
+            pltpu.VMEM(values.shape, jnp.bfloat16),
+            pltpu.VMEM((nodes + 128, width), jnp.float32),
+            pltpu.SemaphoreType.DMA((values.shape[0] // UNROLL,)),
+        ],
+        out_shape=jax.ShapeDtypeStruct(begin.shape, jnp.bfloat16),
+        compiler_params=pltpu.CompilerParams(vmem_limit_bytes=VMEM_TILES),
+        name="last_sum",
+    )(rows, cols, listed, source, begin, pltpu.with_memory_space_constraint(values, pltpu.HBM))
 
 
 def local(
@@ -273,12 +336,12 @@
         selected, wanted = lax.optimization_barrier((selected, wanted))
     received = lax.all_to_all(selected, AXES, split_axis=0, concat_axis=0, tiled=True)
     selected = gather_rows(wanted, features, weight, 1, halves, owners, EARLY, owners, ahead)
-    total = sparse_sum(sparse_rows[0], sparse_cols[0], received, sparse_vals[0], rows_dev, 0, halves)
+    total, picked, listed = first_sum(sparse_rows[0], sparse_cols[0], received, sparse_vals[0], rows_dev)
     received = lax.all_to_all(selected, AXES, split_axis=0, concat_axis=0, tiled=True)
     total = dense_sum(
         dense_rows.reshape(-1), dense_cols.reshape(-1), stripes, dense_vals.reshape(-1, tile, tile), total
     )
-    return sparse_sum(sparse_rows[0], sparse_cols[0], received, sparse_vals[0], rows_dev, 1, halves, total)
+    return last_sum(sparse_rows[0], sparse_cols[0], listed, received, picked, total)
 
 
 def solution(mesh):

time: 205 us -> 204 us (level)
  waiting for transfers between devices: 88.5 us -> 84.8 us
  local copies, waits for them, and re-layouts: 2.17 us -> 5.66 us
    all_gather x1, waiting for transfers between devices: 18.7 us -> 8.62 us  [local(): stripes = lax.all_gather(mine[None], AXES, axis=0, tiled=True)]
    all_to_all x2, waiting for transfers between devices: 48.5 us -> 54.9 us  [local(): lax.all_to_all(selected, AXES, split_axis=0, concat_axis=0, tiled=True)]
    unnamed x8 -> x16, local copies, waits for them, and re-layouts: 0.01 us -> 4.64 us
where the time goes in v5:
time: 204 us; the launch traced here: 203 us
  waiting for transfers between devices  84.8 us (42%)
  Pallas kernels  72.9 us (36%)
  starting transfers between devices  24.6 us (12%)
  between operations  13.6 us (7%)
  local copies, waits for them, and re-layouts  5.66 us (3%)
    all_to_all x2, waiting for transfers between devices, local(): lax.all_to_all(selected, AXES, split_axis=0, concat_axis=0, tiled=True)  54.9 us
    pallas_call x3, Pallas kernels, gather_rows(): pl.pallas_call(functools.partial(gather_kernel, half=half, halves=halves,...  44.1 us
    all_to_all x1, waiting for transfers between devices, local(): lax.all_to_all(message, AXES, split_axis=0, concat_axis=0, tiled=True)  21.3 us
    all_to_all x2, starting transfers between devices, local(): lax.all_to_all(selected, AXES, split_axis=0, concat_axis=0, tiled=True)  13 us
    all_to_all x1, starting transfers between devices, local(): lax.all_to_all(message, AXES, split_axis=0, concat_axis=0, tiled=True)  11.5 us
    pallas_call x1, Pallas kernels, first_sum(): pl.pallas_call(first_kernel, grid_spec=pltpu.PrefetchScalarGridSpec(num_s...  9.63 us
    pallas_call x1, Pallas kernels, dense_sum(): pl.pallas_call(dense_kernel, grid_spec=pltpu.PrefetchScalarGridSpec(num_s...  9.4 us
    all_gather x1, waiting for transfers between devices, local(): stripes = lax.all_gather(mine[None], AXES, axis=0, tiled=True)  8.62 us
  transfers between devices with their start and end apart: 4, of which 4 were waited for; matrix products, arithmetic and copies ran while one was open for 1% of the time, Pallas kernels for 31%

profile of v5, /device:TPU:1, one launch (start us, length us, event | category | flops | bytes accessed | tf_op | source)
XLA Modules:
  0.0 203.2 jit_solution(8869157375583160418)
XLA Ops:
  6.5 0.0 copy-start.7
  6.5 0.0 copy-start.4
  6.5 3.1 %build_message.1 = bf16[128,36,128]{2,1,0:T(8,128)(2,1)} custom-call(bf16[128,32,128]{2,1,0:T(8,128)(2,1)} %bitcast.15, s32[128,256]{1,0:T(8,128)} %bitcast.22, s32[1,128]{1,0:T(1,128)} %counts_ref.1), custom_call_target="tpu_custom_call" | custom-call | tf_op jit(solution)/shard_map/build_message/pallas_call | solution.py:41
  9.6 11.5 %all-to-all-start = ((bf16[128,36,128]{2,1,0:T(8,128)(2,1)}), bf16[128,36,128]{2,1,0:T(8,128)(2,1)S(1)}, u32[]{:S(2)}, u32[]{:S(2)}) async-start(bf16[128,36,128]{2,1,0:T(8,128)(2,1)} %build_message.1), calls=%async_computation | async-start | bytes 2621440 | tf_op jit(solution)/shard_map/all_to_all | solution.py:324
  21.2 0.0 all-gather.3.cloned.1.call-start
  21.2 0.0 copy-done.7
  21.2 21.3 %all-to-all-done = bf16[128,36,128]{2,1,0:T(8,128)(2,1)S(1)} async-done(((bf16[128,36,128]{2,1,0:T(8,128)(2,1)}), bf16[128,36,128]{2,1,0:T(8,128)(2,1)S(1)}, u32[]{:S(2)}, u32[]{:S(2)}) %all-to-all-start) | async-done | bytes 1179680 | tf_op jit(solution)/shard_map/all_to_all | solution.py:324
  42.5 0.1 slice.21
  42.6 0.6 gather_fusion
  43.2 0.0 copy-done.4
  43.2 0.8 convolution_convert_fusion
  44.0 0.0 all-gather.3.cloned.1.call-update
  44.0 0.1 slice_convert_fusion
  44.1 0.2 reshape.36
  44.3 0.8 slice_add_fusion
  45.1 19.3 %gather_rows.3 = bf16[128,128,128]{2,1,0:T(8,128)(2,1)} custom-call(s32[32768]{0:T(1024)} %bitcast.19, bf16[4096,128]{1,0:T(8,128)(2,1)} %features_ref.5, bf16[128,128]{1,0:T(8,128)(2,1)} %weight_ref.5), custom_call_target="tpu_custom_call" | custom-call | tf_op jit(solution)/shard_map/gather_rows/pallas_call | solution.py:85
  64.5 8.7 %gather_rows.4.refs_0_ = bf16[128,128,128]{2,1,0:T(8,128)(2,1)} custom-call(s32[32768]{0:T(1024)} %bitcast.20, bf16[4096,128]{1,0:T(8,128)(2,1)} %features_ref.5, bf16[128,128]{1,0:T(8,128)(2,1)} %weight_ref.5), custom_call_target="tpu_custom_call" | custom-call | tf_op jit(solution)/shard_map/gather_rows/pallas_call | solution.py:85
  73.2 6.0 %all-to-all-start.1 = ((bf16[128,128,128]{2,1,0:T(8,128)(2,1)}), bf16[128,128,128]{2,1,0:T(8,128)(2,1)}, u32[]{:S(2)}, u32[]{:S(2)}) async-start(bf16[128,128,128]{2,1,0:T(8,128)(2,1)} %gather_rows.3), calls=%async_computation.1 | async-start | bytes 8388608 | tf_op jit(solution)/shard_map/all_to_all | solution.py:337
  79.2 16.1 %gather_rows.5 = bf16[128,128,128]{2,1,0:T(8,128)(2,1)} custom-call(s32[32768]{0:T(1024)} %bitcast.21, bf16[4096,128]{1,0:T(8,128)(2,1)} %features_ref.5, bf16[128,128]{1,0:T(8,128)(2,1)} %weight_ref.5, bf16[128,128,128]{2,1,0:T(8,128)(2,1)} %gather_rows.4.refs_0_), custom_call_target="tpu_custom_call", output_to_operand_aliasing={{}: (3, {})} | custom-call | tf_op jit(solution)/shard_map/gather_rows/pallas_call | solution.py:85
  95.3 0.0 copy-start.5
  95.3 0.0 copy-start.6
  95.3 0.0 copy-start.2
  95.3 0.0 copy-start.3
  95.3 35.7 %all-to-all-done.1.source_hbm = bf16[128,128,128]{2,1,0:T(8,128)(2,1)} async-done(((bf16[128,128,128]{2,1,0:T(8,128)(2,1)}), bf16[128,128,128]{2,1,0:T(8,128)(2,1)}, u32[]{:S(2)}, u32[]{:S(2)}) %all-to-all-start.1) | async-done | bytes 4194336 | tf_op jit(solution)/shard_map/all_to_all | solution.py:337
  131.1 7.0 %all-to-all-start.2 = ((bf16[128,128,128]{2,1,0:T(8,128)(2,1)}), bf16[128,128,128]{2,1,0:T(8,128)(2,1)}, u32[]{:S(2)}, u32[]{:S(2)}) async-start(bf16[128,128,128]{2,1,0:T(8,128)(2,1)} %gather_rows.5), calls=%async_computation.2 | async-start | bytes 8388608 | tf_op jit(solution)/shard_map/all_to_all | solution.py:340
  138.1 0.0 copy-done.5
  138.1 0.1 reshape.32.rows_ref
  138.2 0.0 copy-done.6
  138.2 0.1 reshape.33.cols_ref
  138.2 0.0 copy-done.2
  138.2 0.0 copy-done.3
  138.2 9.6 %first_sum.1 = (f32[4096,128]{1,0:T(8,128)S(1)}, bf16[256,128,128]{2,1,0:T(8,128)(2,1)S(1)}, s32[264]{0:T(512)S(1)}) custom-call(s32[256]{0:T(256)S(1)} %bitcast.11, s32[256]{0:T(256)S(1)} %bitcast.13, bf16[128,128,128]{2,1,0:T(8,128)(2,1)} %all-to-all-done.1.source_hbm, bf16[256,128,128]{2,1,0:T(8,128)(2,1)} %bitcast.16), custom_call_target="tpu_custom_call" | custom-call | tf_op jit(solution)/shard_map/first_sum/pallas_call | solution.py:219
  147.9 0.0 copy-start
  147.9 3.2 %copy-done = bf16[256,128,128]{2,1,0:T(8,128)(2,1)} copy-done((bf16[256,128,128]{2,1,0:T(8,128)(2,1)}, bf16[256,128,128]{2,1,0:T(8,128)(2,1)S(1)}, u32[]{:S(2)}) %copy-start) | copy-done | bytes 8388632
  151.1 0.0 copy-start.1
  151.1 1.4 copy-done.1
  152.5 8.6 %all-gather.3.cloned.1.call-done = bf16[1024,32,128]{2,1,0:T(8,128)(2,1)} async-done(((bf16[8,32,128]{2,1,0:T(8,128)(2,1)}), bf16[1024,32,128]{2,1,0:T(8,128)(2,1)}) %all-gather.3.cloned.1.call-update) | async-done | bytes 8388624 | tf_op jit(solution)/shard_map/all_gather | solution.py:327
  161.1 9.4 %dense_sum.1.begin_ref = f32[4096,128]{1,0:T(8,128)S(1)} custom-call(s32[256]{0:T(256)S(1)} %reshape.32.rows_ref, s32[256]{0:T(256)S(1)} %reshape.33.cols_ref, bf16[128,8,32,128]{3,2,1,0:T(8,128)(2,1)} %bitcast.18, bf16[256,128,128]{2,1,0:T(8,128)(2,1)} %bitcast.17, f32[4096,128]{1,0:T(8,128)} %copy-done.1), custom_call_target="tpu_custom_call" | custom-call | tf_op jit(solution)/shard_map/dense_sum/pallas_call | solution.py:148
  170.5 19.2 %all-to-all-done.2.source_ref = bf16[128,128,128]{2,1,0:T(8,128)(2,1)} async-done(((bf16[128,128,128]{2,1,0:T(8,128)(2,1)}), bf16[128,128,128]{2,1,0:T(8,128)(2,1)}, u32[]{:S(2)}, u32[]{:S(2)}) %all-to-all-start.2) | async-done | bytes 4194336 | tf_op jit(solution)/shard_map/all_to_all | solution.py:340
  189.7 6.6 %last_sum.1 = bf16[4096,128]{1,0:T(8,128)(2,1)} custom-call(s32[256]{0:T(256)S(1)} %bitcast.12, s32[256]{0:T(256)S(1)} %bitcast.14, s32[264]{0:T(512)S(1)} %get-tuple-element.12.list_ref, bf16[128,128,128]{2,1,0:T(8,128)(2,1)} %all-to-all-done.2.source_ref, f32[4096,128]{1,0:T(8,128)S(1)} %dense_sum.1.begin_ref, bf16[256,128,128]{2,1,0:T(8,128)(2,1)} %copy-done), custom_call_target="tpu_custom_call" | custom-call | tf_op jit(solution)/shard_map/last_sum/pallas_call | solution.py:289
  (3 shorter events, 0.0 us)
Async XLA Ops:
  6.5 14.7 %copy-start.7 = (s32[8]{0:T(128)S(1)}, s32[8]{0:T(128)}, u32[]{:S(2)}) copy-start(s32[8]{0:T(128)} %param.13) | copy-start | bytes 100
  6.5 36.6 %copy-start.4 = (bf16[128,128]{1,0:T(8,128)(2,1)S(1)}, bf16[128,128]{1,0:T(8,128)(2,1)}, u32[]{:S(2)}) copy-start(bf16[128,128]{1,0:T(8,128)(2,1)} %weight_ref.5) | copy-start | bytes 98308
  9.6 32.9 %all-to-all-start = ((bf16[128,36,128]{2,1,0:T(8,128)(2,1)}), bf16[128,36,128]{2,1,0:T(8,128)(2,1)S(1)}, u32[]{:S(2)}, u32[]{:S(2)}) async-start(bf16[128,36,128]{2,1,0:T(8,128)(2,1)} %build_message.1), calls=%async_computation | async-start | bytes 2621440 | tf_op jit(solution)/shard_map/all_to_all | solution.py:324
  21.2 140.0 %all-gather.3.cloned.1.call-start = ((), (), s32[]{:S(2)}) async-start(), calls=%async_computation.3 | async-start | bytes 8454144 | tf_op jit(solution)/shard_map/all_gather | solution.py:327
  73.2 57.9 %all-to-all-start.1 = ((bf16[128,128,128]{2,1,0:T(8,128)(2,1)}), bf16[128,128,128]{2,1,0:T(8,128)(2,1)}, u32[]{:S(2)}, u32[]{:S(2)}) async-start(bf16[128,128,128]{2,1,0:T(8,128)(2,1)} %gather_rows.3), calls=%async_computation.1 | async-start | bytes 8388608 | tf_op jit(solution)/shard_map/all_to_all | solution.py:337
  95.3 42.8 %copy-start.5 = (s32[1,8,32]{2,1,0:T(8,128)S(1)}, s32[1,8,32]{2,1,0:T(8,128)}, u32[]{:S(2)}) copy-start(s32[1,8,32]{2,1,0:T(8,128)} %param.15) | copy-start | bytes 3076
  95.3 42.9 %copy-start.6 = (s32[1,8,32]{2,1,0:T(8,128)S(1)}, s32[1,8,32]{2,1,0:T(8,128)}, u32[]{:S(2)}) copy-start(s32[1,8,32]{2,1,0:T(8,128)} %param.16) | copy-start | bytes 3076
  95.3 42.9 %copy-start.2 = (s32[1,256]{1,0:T(1,128)S(1)}, s32[1,256]{1,0:T(1,128)}, u32[]{:S(2)}) copy-start(s32[1,256]{1,0:T(1,128)} %param.18) | copy-start | bytes 3076
  95.3 42.9 %copy-start.3 = (s32[1,256]{1,0:T(1,128)S(1)}, s32[1,256]{1,0:T(1,128)}, u32[]{:S(2)}) copy-start(s32[1,256]{1,0:T(1,128)} %param.19) | copy-start | bytes 3076
  131.1 58.7 %all-to-all-start.2 = ((bf16[128,128,128]{2,1,0:T(8,128)(2,1)}), bf16[128,128,128]{2,1,0:T(8,128)(2,1)}, u32[]{:S(2)}, u32[]{:S(2)}) async-start(bf16[128,128,128]{2,1,0:T(8,128)(2,1)} %gather_rows.5), calls=%async_computation.2 | async-start | bytes 8388608 | tf_op jit(solution)/shard_map/all_to_all | solution.py:340
  147.9 3.2 %copy-start = (bf16[256,128,128]{2,1,0:T(8,128)(2,1)}, bf16[256,128,128]{2,1,0:T(8,128)(2,1)S(1)}, u32[]{:S(2)}) copy-start(bf16[256,128,128]{2,1,0:T(8,128)(2,1)S(1)} %get-tuple-element.16.values_ref) | copy-start | bytes 25165828
  151.1 1.4 copy-start.1
Sparse Core Ops, SparseCore 0:
  44.2 116.9 all-gather.2

commit v6 on v5

--- a/solution.py
+++ b/solution.py
@@ -257,17 +257,19 @@
         at = pl.ds(part * UNROLL, UNROLL)
         return pltpu.make_async_copy(values_ref.at[at], held_ref.at[at], value_sems.at[part])
 
-    for part in range(count // UNROLL):
-
+    def start_values(part):
         @pl.when(part * UNROLL < taken)
         def _():
             load_values(part).start()
 
+    start_values(0)
+    start_values(1)
     total_ref[pl.ds(0, nodes), :] = begin_ref[...]
     total_ref[pl.ds(nodes, 128), :] = jnp.zeros((128, total_ref.shape[1]), jnp.float32)
 
     def group(step, carry):
         load_values(step).wait()
+        start_values(step + 2)
         for j in range(UNROLL):
             entry = jnp.minimum(step * UNROLL + j, taken - 1)
             k = list_ref[entry]

time: 204 us -> 205 us (level)
  no operation moved by 1% of the time
where the time goes in v6:
time: 205 us; the launch traced here: 204 us
  waiting for transfers between devices  85.3 us (42%)
  Pallas kernels  73.5 us (36%)
  starting transfers between devices  24.6 us (12%)
  between operations  13.6 us (7%)
  local copies, waits for them, and re-layouts  5.66 us (3%)
    all_to_all x2, waiting for transfers between devices, local(): lax.all_to_all(selected, AXES, split_axis=0, concat_axis=0, tiled=True)  54.9 us
    pallas_call x3, Pallas kernels, gather_rows(): pl.pallas_call(functools.partial(gather_kernel, half=half, halves=halves,...  44.1 us
    all_to_all x1, waiting for transfers between devices, local(): lax.all_to_all(message, AXES, split_axis=0, concat_axis=0, tiled=True)  21.3 us
    all_to_all x2, starting transfers between devices, local(): lax.all_to_all(selected, AXES, split_axis=0, concat_axis=0, tiled=True)  13 us
    all_to_all x1, starting transfers between devices, local(): lax.all_to_all(message, AXES, split_axis=0, concat_axis=0, tiled=True)  11.5 us
    pallas_call x1, Pallas kernels, dense_sum(): pl.pallas_call(dense_kernel, grid_spec=pltpu.PrefetchScalarGridSpec(num_s...  9.42 us
    pallas_call x1, Pallas kernels, first_sum(): pl.pallas_call(first_kernel, grid_spec=pltpu.PrefetchScalarGridSpec(num_s...  9.19 us
    all_gather x1, waiting for transfers between devices, local(): stripes = lax.all_gather(mine[None], AXES, axis=0, tiled=True)  9.05 us
  transfers between devices with their start and end apart: 4, of which 4 were waited for; matrix products, arithmetic and copies ran while one was open for 1% of the time, Pallas kernels for 31%

profile of v6, /device:TPU:1, one launch (start us, length us, event | category | flops | bytes accessed | tf_op | source)
XLA Modules:
  0.0 204.3 jit_solution(9048960742403986168)
XLA Ops:
  6.5 0.0 copy-start.7
  6.5 0.0 copy-start.4
  6.5 3.1 %build_message.1 = bf16[128,36,128]{2,1,0:T(8,128)(2,1)} custom-call(bf16[128,32,128]{2,1,0:T(8,128)(2,1)} %bitcast.15, s32[128,256]{1,0:T(8,128)} %bitcast.22, s32[1,128]{1,0:T(1,128)} %counts_ref.1), custom_call_target="tpu_custom_call" | custom-call | tf_op jit(solution)/shard_map/build_message/pallas_call | solution.py:41
  9.6 11.5 %all-to-all-start = ((bf16[128,36,128]{2,1,0:T(8,128)(2,1)}), bf16[128,36,128]{2,1,0:T(8,128)(2,1)S(1)}, u32[]{:S(2)}, u32[]{:S(2)}) async-start(bf16[128,36,128]{2,1,0:T(8,128)(2,1)} %build_message.1), calls=%async_computation | async-start | bytes 2621440 | tf_op jit(solution)/shard_map/all_to_all | solution.py:326
  21.2 0.0 all-gather.3.cloned.1.call-start
  21.2 0.0 copy-done.7
  21.2 21.3 %all-to-all-done = bf16[128,36,128]{2,1,0:T(8,128)(2,1)S(1)} async-done(((bf16[128,36,128]{2,1,0:T(8,128)(2,1)}), bf16[128,36,128]{2,1,0:T(8,128)(2,1)S(1)}, u32[]{:S(2)}, u32[]{:S(2)}) %all-to-all-start) | async-done | bytes 1179680 | tf_op jit(solution)/shard_map/all_to_all | solution.py:326
  42.5 0.1 slice.21
  42.6 0.6 gather_fusion
  43.2 0.0 copy-done.4
  43.2 0.8 convolution_convert_fusion
  44.0 0.0 all-gather.3.cloned.1.call-update
  44.0 0.1 slice_convert_fusion
  44.1 0.2 reshape.36
  44.3 0.8 slice_add_fusion
  45.1 19.3 %gather_rows.3 = bf16[128,128,128]{2,1,0:T(8,128)(2,1)} custom-call(s32[32768]{0:T(1024)} %bitcast.19, bf16[4096,128]{1,0:T(8,128)(2,1)} %features_ref.5, bf16[128,128]{1,0:T(8,128)(2,1)} %weight_ref.5), custom_call_target="tpu_custom_call" | custom-call | tf_op jit(solution)/shard_map/gather_rows/pallas_call | solution.py:85
  64.5 8.7 %gather_rows.4.refs_0_ = bf16[128,128,128]{2,1,0:T(8,128)(2,1)} custom-call(s32[32768]{0:T(1024)} %bitcast.20, bf16[4096,128]{1,0:T(8,128)(2,1)} %features_ref.5, bf16[128,128]{1,0:T(8,128)(2,1)} %weight_ref.5), custom_call_target="tpu_custom_call" | custom-call | tf_op jit(solution)/shard_map/gather_rows/pallas_call | solution.py:85
  73.2 6.0 %all-to-all-start.1 = ((bf16[128,128,128]{2,1,0:T(8,128)(2,1)}), bf16[128,128,128]{2,1,0:T(8,128)(2,1)}, u32[]{:S(2)}, u32[]{:S(2)}) async-start(bf16[128,128,128]{2,1,0:T(8,128)(2,1)} %gather_rows.3), calls=%async_computation.1 | async-start | bytes 8388608 | tf_op jit(solution)/shard_map/all_to_all | solution.py:339
  79.2 16.1 %gather_rows.5 = bf16[128,128,128]{2,1,0:T(8,128)(2,1)} custom-call(s32[32768]{0:T(1024)} %bitcast.21, bf16[4096,128]{1,0:T(8,128)(2,1)} %features_ref.5, bf16[128,128]{1,0:T(8,128)(2,1)} %weight_ref.5, bf16[128,128,128]{2,1,0:T(8,128)(2,1)} %gather_rows.4.refs_0_), custom_call_target="tpu_custom_call", output_to_operand_aliasing={{}: (3, {})} | custom-call | tf_op jit(solution)/shard_map/gather_rows/pallas_call | solution.py:85
  95.3 0.0 copy-start.5
  95.3 0.0 copy-start.6
  95.3 0.0 copy-start.2
  95.3 0.0 copy-start.3
  95.3 35.7 %all-to-all-done.1.source_hbm = bf16[128,128,128]{2,1,0:T(8,128)(2,1)} async-done(((bf16[128,128,128]{2,1,0:T(8,128)(2,1)}), bf16[128,128,128]{2,1,0:T(8,128)(2,1)}, u32[]{:S(2)}, u32[]{:S(2)}) %all-to-all-start.1) | async-done | bytes 4194336 | tf_op jit(solution)/shard_map/all_to_all | solution.py:339
  131.1 7.0 %all-to-all-start.2 = ((bf16[128,128,128]{2,1,0:T(8,128)(2,1)}), bf16[128,128,128]{2,1,0:T(8,128)(2,1)}, u32[]{:S(2)}, u32[]{:S(2)}) async-start(bf16[128,128,128]{2,1,0:T(8,128)(2,1)} %gather_rows.5), calls=%async_computation.2 | async-start | bytes 8388608 | tf_op jit(solution)/shard_map/all_to_all | solution.py:342
  138.1 0.0 copy-done.5
  138.1 0.1 reshape.32.rows_ref
  138.2 0.0 copy-done.6
  138.2 0.1 reshape.33.cols_ref
  138.2 0.0 copy-done.2
  138.2 0.0 copy-done.3
  138.2 9.2 %first_sum.1 = (f32[4096,128]{1,0:T(8,128)S(1)}, bf16[256,128,128]{2,1,0:T(8,128)(2,1)S(1)}, s32[264]{0:T(512)S(1)}) custom-call(s32[256]{0:T(256)S(1)} %bitcast.11, s32[256]{0:T(256)S(1)} %bitcast.13, bf16[128,128,128]{2,1,0:T(8,128)(2,1)} %all-to-all-done.1.source_hbm, bf16[256,128,128]{2,1,0:T(8,128)(2,1)} %bitcast.16), custom_call_target="tpu_custom_call" | custom-call | tf_op jit(solution)/shard_map/first_sum/pallas_call | solution.py:219
  147.4 0.0 copy-start
  147.5 3.2 %copy-done = bf16[256,128,128]{2,1,0:T(8,128)(2,1)} copy-done((bf16[256,128,128]{2,1,0:T(8,128)(2,1)}, bf16[256,128,128]{2,1,0:T(8,128)(2,1)S(1)}, u32[]{:S(2)}) %copy-start) | copy-done | bytes 8388632
  150.7 0.0 copy-start.1
  150.7 1.4 copy-done.1
  152.1 9.1 %all-gather.3.cloned.1.call-done = bf16[1024,32,128]{2,1,0:T(8,128)(2,1)} async-done(((bf16[8,32,128]{2,1,0:T(8,128)(2,1)}), bf16[1024,32,128]{2,1,0:T(8,128)(2,1)}) %all-gather.3.cloned.1.call-update) | async-done | bytes 8388624 | tf_op jit(solution)/shard_map/all_gather | solution.py:329
  161.1 9.4 %dense_sum.1.begin_ref = f32[4096,128]{1,0:T(8,128)S(1)} custom-call(s32[256]{0:T(256)S(1)} %reshape.32.rows_ref, s32[256]{0:T(256)S(1)} %reshape.33.cols_ref, bf16[128,8,32,128]{3,2,1,0:T(8,128)(2,1)} %bitcast.18, bf16[256,128,128]{2,1,0:T(8,128)(2,1)} %bitcast.17, f32[4096,128]{1,0:T(8,128)} %copy-done.1), custom_call_target="tpu_custom_call" | custom-call | tf_op jit(solution)/shard_map/dense_sum/pallas_call | solution.py:148
  170.6 19.2 %all-to-all-done.2.source_ref = bf16[128,128,128]{2,1,0:T(8,128)(2,1)} async-done(((bf16[128,128,128]{2,1,0:T(8,128)(2,1)}), bf16[128,128,128]{2,1,0:T(8,128)(2,1)}, u32[]{:S(2)}, u32[]{:S(2)}) %all-to-all-start.2) | async-done | bytes 4194336 | tf_op jit(solution)/shard_map/all_to_all | solution.py:342
  189.7 7.7 %last_sum.1 = bf16[4096,128]{1,0:T(8,128)(2,1)} custom-call(s32[256]{0:T(256)S(1)} %bitcast.12, s32[256]{0:T(256)S(1)} %bitcast.14, s32[264]{0:T(512)S(1)} %get-tuple-element.12.list_ref, bf16[128,128,128]{2,1,0:T(8,128)(2,1)} %all-to-all-done.2.source_ref, f32[4096,128]{1,0:T(8,128)S(1)} %dense_sum.1.begin_ref, bf16[256,128,128]{2,1,0:T(8,128)(2,1)} %copy-done), custom_call_target="tpu_custom_call" | custom-call | tf_op jit(solution)/shard_map/last_sum/pallas_call | solution.py:291
  (3 shorter events, 0.0 us)
Async XLA Ops:
  6.5 14.7 %copy-start.7 = (s32[8]{0:T(128)S(1)}, s32[8]{0:T(128)}, u32[]{:S(2)}) copy-start(s32[8]{0:T(128)} %param.13) | copy-start | bytes 100
  6.5 36.6 %copy-start.4 = (bf16[128,128]{1,0:T(8,128)(2,1)S(1)}, bf16[128,128]{1,0:T(8,128)(2,1)}, u32[]{:S(2)}) copy-start(bf16[128,128]{1,0:T(8,128)(2,1)} %weight_ref.5) | copy-start | bytes 98308
  9.6 32.9 %all-to-all-start = ((bf16[128,36,128]{2,1,0:T(8,128)(2,1)}), bf16[128,36,128]{2,1,0:T(8,128)(2,1)S(1)}, u32[]{:S(2)}, u32[]{:S(2)}) async-start(bf16[128,36,128]{2,1,0:T(8,128)(2,1)} %build_message.1), calls=%async_computation | async-start | bytes 2621440 | tf_op jit(solution)/shard_map/all_to_all | solution.py:326
  21.2 140.0 %all-gather.3.cloned.1.call-start = ((), (), s32[]{:S(2)}) async-start(), calls=%async_computation.3 | async-start | bytes 8454144 | tf_op jit(solution)/shard_map/all_gather | solution.py:329
  73.2 57.9 %all-to-all-start.1 = ((bf16[128,128,128]{2,1,0:T(8,128)(2,1)}), bf16[128,128,128]{2,1,0:T(8,128)(2,1)}, u32[]{:S(2)}, u32[]{:S(2)}) async-start(bf16[128,128,128]{2,1,0:T(8,128)(2,1)} %gather_rows.3), calls=%async_computation.1 | async-start | bytes 8388608 | tf_op jit(solution)/shard_map/all_to_all | solution.py:339
  95.3 42.8 %copy-start.5 = (s32[1,8,32]{2,1,0:T(8,128)S(1)}, s32[1,8,32]{2,1,0:T(8,128)}, u32[]{:S(2)}) copy-start(s32[1,8,32]{2,1,0:T(8,128)} %param.15) | copy-start | bytes 3076
  95.3 42.9 %copy-start.6 = (s32[1,8,32]{2,1,0:T(8,128)S(1)}, s32[1,8,32]{2,1,0:T(8,128)}, u32[]{:S(2)}) copy-start(s32[1,8,32]{2,1,0:T(8,128)} %param.16) | copy-start | bytes 3076
  95.3 42.9 %copy-start.2 = (s32[1,256]{1,0:T(1,128)S(1)}, s32[1,256]{1,0:T(1,128)}, u32[]{:S(2)}) copy-start(s32[1,256]{1,0:T(1,128)} %param.18) | copy-start | bytes 3076
  95.3 42.9 %copy-start.3 = (s32[1,256]{1,0:T(1,128)S(1)}, s32[1,256]{1,0:T(1,128)}, u32[]{:S(2)}) copy-start(s32[1,256]{1,0:T(1,128)} %param.19) | copy-start | bytes 3076
  131.1 58.7 %all-to-all-start.2 = ((bf16[128,128,128]{2,1,0:T(8,128)(2,1)}), bf16[128,128,128]{2,1,0:T(8,128)(2,1)}, u32[]{:S(2)}, u32[]{:S(2)}) async-start(bf16[128,128,128]{2,1,0:T(8,128)(2,1)} %gather_rows.5), calls=%async_computation.2 | async-start | bytes 8388608 | tf_op jit(solution)/shard_map/all_to_all | solution.py:342
  147.4 3.2 %copy-start = (bf16[256,128,128]{2,1,0:T(8,128)(2,1)}, bf16[256,128,128]{2,1,0:T(8,128)(2,1)S(1)}, u32[]{:S(2)}) copy-start(bf16[256,128,128]{2,1,0:T(8,128)(2,1)S(1)} %get-tuple-element.16.values_ref) | copy-start | bytes 25165828
  150.7 1.4 copy-start.1
Sparse Core Ops, SparseCore 0:
  44.2 116.9 all-gather.2
